TPU v7x, 32 devices: a whole 2x2x4 slice. The times are simulated.
32 devices in a mesh: dp: 4 (over z), expert: 8 (over y, x, core).
Axes of the slice: x: 2, y: 2, z: 4, core: 2. Of those that a mesh axis runs over, the one named last changes fastest.
Arguments:
- grad_out: bfloat16 [4096, 2880], P(('dp', 'expert')), may hold values from -96 to 96
- hidden_act: bfloat16 [4096, 4, 360], P(('dp', 'expert')), may hold values from -6 to 6
- gate_weights: bfloat16 [4096, 4], P(('dp', 'expert')), may hold values from 0.099609375 to 0.69921875
- routing: int32 [4096, 4], P(('dp', 'expert')), may hold values from 0 to 7, all different within a row; in each aligned block of 128 rows (0 to 127, 128 to 255, ...) at most 80 rows name the same one
- resp_lengths: int32 [32, 4], P(('dp', 'expert')), may hold values from 1 to 64, 128 in all within a row
- advantage: float32 [32, 4], P(('dp', 'expert')), may hold values from -4 to 4
- w_down: bfloat16 [8, 360, 2880], P('expert', None, 'dp'), may hold values from -0.3125 to 0.3125
Outputs:
- grad_down: float32 [8, 360, 2880], P('expert', None, 'dp')
- grad_hidden: float32 [4096, 4, 360], P(('dp', 'expert'))
- grad_gates: float32 [4096, 4], P(('dp', 'expert'))
Inputs may be any that keep to these rules, and one draw needn't show every extreme that they name: `routing`: each token names 4 different experts; within the 128 tokens of one device no expert is named more than 80 times, a bound that some block reaches. `resp_lengths`: the 4 lengths of one device add up to 128; the largest is 64.
All inputs are finite; a program needn't handle non-finite values.
Results may differ from a plain program's by a relative error of at most 0.0041.
Values may be sent and summed in bfloat16 or wider, within the bound.
A program may use at most 64 MiB of HBM per device.

v0:
```python
import jax
import jax.numpy as jnp
from jax import lax
from jax.sharding import PartitionSpec as P


def weight_terms(hid_recv, gated):
    partial_term = lax.dot_general(
        hid_recv, gated, (((0,), (0,)), ((), ())), preferred_element_type=jnp.float32
    )
    return lax.psum_scatter(partial_term, "dp", scatter_dimension=1, tiled=True)[None]


def local(grad_out, hidden_act, gate_weights, routing, resp_lengths, advantage, w_down):
    rows = grad_out.shape[0]
    width = grad_out.shape[1]
    topk = routing.shape[1]
    ffw = hidden_act.shape[2]
    nexp = lax.axis_size("expert")
    cap = min(rows, 5 * rows * topk // (4 * nexp))
    items = rows * topk
    slots = nexp * cap
    ends = jnp.cumsum(resp_lengths[0])
    starts = ends - resp_lengths[0]
    position = jnp.arange(rows, dtype=jnp.int32)
    inside = (position[:, None] >= starts[None, :]) & (position[:, None] < ends[None, :])
    ratio = advantage[0] / resp_lengths[0].astype(jnp.float32)
    scale = jnp.sum(jnp.where(inside, ratio[None, :], 0.0), axis=1)
    cotan = (scale[:, None] * grad_out.astype(jnp.float32)).astype(jnp.bfloat16)
    dest = routing.reshape(-1)
    onehot = (dest[:, None] == jnp.arange(nexp, dtype=jnp.int32)[None, :]).astype(jnp.int32)
    rank = jnp.cumsum(onehot, axis=0) - onehot
    place = jnp.sum(rank * onehot, axis=1)
    flat = dest * cap + place
    slot_item = (
        jnp.full((slots,), items, jnp.int32).at[flat].set(jnp.arange(items, dtype=jnp.int32))
    )
    valid = slot_item < items
    safe = jnp.minimum(slot_item, items - 1)
    send_cot = jnp.where(valid[:, None], cotan[safe // topk], jnp.zeros((), jnp.bfloat16))
    send_hid = jnp.where(
        valid[:, None], hidden_act.reshape(items, ffw)[safe], jnp.zeros((), jnp.bfloat16)
    )
    send_gate = jnp.where(valid, gate_weights.reshape(items)[safe], jnp.zeros((), jnp.bfloat16))
    recv_cot, recv_hid, recv_gate = (
        lax.all_to_all(
            send_cot.reshape(nexp, cap, width), "expert", split_axis=0, concat_axis=0, tiled=True
        ),
        lax.all_to_all(
            send_hid.reshape(nexp, cap, ffw), "expert", split_axis=0, concat_axis=0, tiled=True
        ),
        lax.all_to_all(
            send_gate.reshape(nexp, cap), "expert", split_axis=0, concat_axis=0, tiled=True
        ),
    )
    recv_cot = recv_cot.reshape(slots, width)
    recv_hid = recv_hid.reshape(slots, ffw)
    recv_gate = recv_gate.reshape(slots).astype(jnp.float32)
    gated = (recv_gate[:, None] * recv_cot.astype(jnp.float32)).astype(jnp.bfloat16)
    local_weight = w_down[0]
    piece = lax.all_gather(local_weight, "dp", axis=1, tiled=True)
    back_sum = lax.dot_general(
        recv_cot, piece, (((1,), (1,)), ((), ())), preferred_element_type=jnp.float32
    )
    output = jnp.dot(recv_hid, piece, preferred_element_type=jnp.float32)
    gate_sum = jnp.sum(recv_cot.astype(jnp.float32) * output, axis=1)
    dhid = recv_gate[:, None] * back_sum
    result_hid, result_gate = (
        lax.all_to_all(
            dhid.reshape(nexp, cap, ffw), "expert", split_axis=0, concat_axis=0, tiled=True
        ),
        lax.all_to_all(
            gate_sum.reshape(nexp, cap), "expert", split_axis=0, concat_axis=0, tiled=True
        ),
    )
    grad_down = weight_terms(recv_hid, gated)
    grad_hidden = result_hid.reshape(slots, ffw)[flat].reshape(rows, topk, ffw)
    grad_gates = result_gate.reshape(slots)[flat].reshape(rows, topk)
    return (grad_down, grad_hidden, grad_gates)


def solution(mesh):
    placed = (
        P(("dp", "expert"), None),
        P(("dp", "expert"), None, None),
        P(("dp", "expert"), None),
        P(("dp", "expert"), None),
        P(("dp", "expert"), None),
        P(("dp", "expert"), None),
        P("expert", None, "dp"),
    )
    return jax.shard_map(
        local,
        mesh=mesh,
        in_specs=placed,
        out_specs=(
            P("expert", None, "dp"),
            P(("dp", "expert"), None, None),
            P(("dp", "expert"), None),
        ),
        check_vma=False,
    )
```

profile of v0, /device:TPU:0, one launch (start us, length us, event | category | flops | bytes accessed | tf_op | source)
XLA Modules:
  0.0 235.0 jit_solution(9380406991646275396)
XLA Ops:
  7.2 0.7 broadcast_multiply_fusion
  7.8 0.8 copy.63
  8.9 0.8 copy.66
  9.7 0.1 reshape.133
  9.8 0.1 copy.62
  10.0 1.1 reduce-window.10
  11.2 0.2 slice_reduce_fusion
  11.5 2.4 %scatter_custom_fusion = s32[640]{0:T(1024)S(1)} fusion(s32[512]{0:T(512)S(1)} %bitcast.52, s32[512]{0:T(512)S(1)} %iota.15, s32[]{:T(128)} %constant.15.clone.1), kind=kCustom, calls=%fused_computation.41 | custom fusion | bytes 2564 | tf_op jit(solution)/shard_map/scatter | solution.py:36
  14.0 4.3 %gather_fusion.1 = bf16[640]{0:T(1024)(128)(2,1)S(1)} fusion(bf16[512]{0:T(512)(128)(2,1)S(1)} %reshape.133, s32[1024]{0:T(1024)S(1)} %get-tuple-element.26), kind=kCustom, calls=%fused_computation.1 | custom fusion | bytes 5120 | tf_op jit(solution)/shard_map/gather | solution.py:44
  18.4 0.7 all_to_all.28
  19.0 5.2 %all-to-all-start.1 = ((bf16[8,1,80]{2,1,0:T(2,128)(2,1)}), bf16[8,1,80]{2,1,0:T(2,128)(2,1)S(1)}, u32[]{:S(2)}, u32[]{:S(2)}) async-start(bf16[8,1,80]{2,1,0:T(2,128)(2,1)} %all_to_all.28), calls=%async_computation.1 | async-start | bytes 8192 | tf_op jit(solution)/shard_map/all_to_all | solution.py:52
  24.2 0.8 reduce-window.14
  25.0 0.7 fusion.15
  25.7 0.7 fusion.16
  26.5 1.2 copy.65
  27.7 0.2 reshape.132
  27.9 2.9 %gather_fusion = bf16[640,360]{1,0:T(8,128)(2,1)S(1)} fusion(bf16[512,360]{1,0:T(8,128)(2,1)S(1)} %reshape.132, s32[1024]{0:T(1024)S(1)} %get-tuple-element.26), kind=kCustom, calls=%fused_computation | custom fusion | bytes 924160 | tf_op jit(solution)/shard_map/gather | solution.py:42
  30.9 0.1 multiply_convert_fusion.2
  31.0 0.9 broadcast_select_fusion.1
  31.9 0.3 copy.68
  32.3 4.6 %gather_fusion.2 = bf16[640,2880]{1,0:T(8,128)(2,1)} fusion(bf16[128,2880]{1,0:T(8,128)(2,1)S(1)} %copy.68, s32[1024]{0:T(1024)S(1)} %get-tuple-element.25), kind=kCustom, calls=%fused_computation.2 | custom fusion | bytes 7375360 | tf_op jit(solution)/shard_map/gather | solution.py:40
  36.9 4.2 %all-to-all-start = ((bf16[8,80,360]{2,1,0:T(8,128)(2,1)}), bf16[8,80,360]{2,1,0:T(8,128)(2,1)S(1)}, u32[]{:S(2)}, u32[]{:S(2)}) async-start(bf16[8,80,360]{2,1,0:T(8,128)(2,1)} %broadcast_select_fusion.1), calls=%async_computation | async-start | bytes 983040 | tf_op jit(solution)/shard_map/all_to_all | solution.py:49
  41.1 4.3 %broadcast_select_fusion = bf16[8,80,2880]{2,1,0:T(8,128)(2,1)} fusion(bf16[8,80,2880]{2,1,0:T(8,128)(2,1)} %bitcast.46, pred[8,80]{1,0:T(8,128)(4,1)S(1)} %broadcast_in_dim.68), kind=kLoop, calls=%fused_computation.10 | loop fusion | flops 1843200 | bytes 7373440 | tf_op jit(solution)/shard_map/jit(_where)/select_n | solution.py:40
  45.4 5.1 %all-to-all-done = bf16[8,80,360]{2,1,0:T(8,128)(2,1)S(1)} async-done(((bf16[8,80,360]{2,1,0:T(8,128)(2,1)}), bf16[8,80,360]{2,1,0:T(8,128)(2,1)S(1)}, u32[]{:S(2)}, u32[]{:S(2)}) %all-to-all-start) | async-done | bytes 460832 | tf_op jit(solution)/shard_map/all_to_all | solution.py:49
  50.5 4.6 %all-to-all-start.2 = ((bf16[8,80,2880]{2,1,0:T(8,128)(2,1)}), bf16[8,80,2880]{2,1,0:T(8,128)(2,1)}, u32[]{:S(2)}, u32[]{:S(2)}) async-start(bf16[8,80,2880]{2,1,0:T(8,128)(2,1)} %broadcast_select_fusion), calls=%async_computation.2 | async-start | bytes 7536640 | tf_op jit(solution)/shard_map/all_to_all | solution.py:46
  55.1 2.7 %copy.69 = bf16[1,360,720]{1,0,2:T(2,128)(2,1)} copy(bf16[1,360,720]{2,1,0:T(8,128)(2,1)S(1)} %copy-done.1) | data formatting | bytes 1036800 | tf_op args[6]
  57.9 0.2 reduce-scatter.4.cloned.1.call-start
  58.1 41.5 %all-to-all-done.2 = bf16[8,80,2880]{2,1,0:T(8,128)(2,1)} async-done(((bf16[8,80,2880]{2,1,0:T(8,128)(2,1)}), bf16[8,80,2880]{2,1,0:T(8,128)(2,1)}, u32[]{:S(2)}, u32[]{:S(2)}) %all-to-all-start.2) | async-done | bytes 3686432 | tf_op jit(solution)/shard_map/all_to_all | solution.py:46
  99.6 6.5 %convolution_bitcast_fusion = f32[2880,360]{1,0:T(8,128)} fusion(bf16[8,80,360]{2,1,0:T(8,128)(2,1)S(1)} %all-to-all-done, bf16[8,80,2880]{2,1,0:T(8,128)(2,1)} %all-to-all-done.2, f32[8,80]{1,0:T(8,128)S(1)} %bitcast.51), kind=kOutput, calls=%fused_computation.8 | convolution fusion | flops 1332633600 | bytes 8296960 | tf_op jit(solution)/shard_map/dot_general | solution.py:8
  106.2 38.0 %all-gather.3.cloned.1.call-done = bf16[1,360,2880]{1,0,2:T(2,128)(2,1)} async-done(((bf16[1,360,720]{1,0,2:T(2,128)(2,1)}), bf16[1,360,2880]{1,0,2:T(2,128)(2,1)}) %all-gather.3.cloned.1.call-update) | async-done | bytes 2073616 | tf_op jit(solution)/shard_map/all_gather | solution.py:61
  144.2 11.1 %copy.70 = bf16[1,360,2880]{2,1,0:T(8,128)(2,1)S(1)} copy(bf16[1,360,2880]{1,0,2:T(2,128)(2,1)} %all-gather.3.cloned.1.call-done) | data formatting | bytes 4147200 | tf_op jit(solution)/shard_map/all_gather | solution.py:61
  155.4 5.9 %copy.72 = bf16[640,2880]{0,1:T(8,128)(2,1)} copy(bf16[640,2880]{1,0:T(8,128)(2,1)} %bitcast.14) | data formatting | bytes 7372800 | tf_op jit(solution)/shard_map/reshape | solution.py:56
  161.3 4.4 %multiply_reduce_fusion = f32[640]{0:T(1024)S(1)} fusion(bf16[640,2880]{0,1:T(8,128)(2,1)} %copy.72, bf16[640,360]{1,0:T(8,128)(2,1)S(1)} %bitcast.48, bf16[1,360,2880]{2,1,0:T(8,128)(2,1)S(1)} %copy.70), kind=kOutput, calls=%fused_computation.7 | convolution fusion | flops 1332632960 | bytes 6223360 | tf_op jit(solution)/shard_map/dot_general | solution.py:65
  165.7 0.7 all_to_all.26
  166.4 3.7 %all-to-all-start.4 = ((f32[8,1,80]{2,1,0:T(1,128)}), f32[8,1,80]{2,1,0:T(1,128)S(1)}, u32[]{:S(2)}, u32[]{:S(2)}) async-start(f32[8,1,80]{2,1,0:T(1,128)} %all_to_all.26), calls=%async_computation.4 | async-start | bytes 8192 | tf_op jit(solution)/shard_map/all_to_all | solution.py:72
  170.1 4.0 %fusion.4 = f32[640,360]{0,1:T(8,128)S(1)} fusion(bf16[640,2880]{1,0:T(8,128)(2,1)} %bitcast.14, bf16[1,360,2880]{2,1,0:T(8,128)(2,1)S(1)} %copy.70, f32[640]{0:T(1024)S(1)} %reshape.144), kind=kOutput, calls=%fused_computation.15 | convolution fusion | flops 1327334400 | bytes 6684160 | tf_op jit(solution)/shard_map/dot_general | solution.py:62
  174.0 1.3 copy.71
  175.3 4.2 %all-to-all-start.3 = ((f32[8,80,360]{2,1,0:T(8,128)}), f32[8,80,360]{2,1,0:T(8,128)S(1)}, u32[]{:S(2)}, u32[]{:S(2)}) async-start(f32[8,80,360]{2,1,0:T(8,128)} %bitcast.16), calls=%async_computation.3 | async-start | bytes 1966080 | tf_op jit(solution)/shard_map/all_to_all | solution.py:69
  179.5 0.5 broadcast.102
  180.1 0.7 reduce.9
  180.8 2.3 gather_fusion.4
  183.2 0.7 copy.74
  183.9 10.4 %all-to-all-done.3 = f32[8,80,360]{2,1,0:T(8,128)S(1)} async-done(((f32[8,80,360]{2,1,0:T(8,128)}), f32[8,80,360]{2,1,0:T(8,128)S(1)}, u32[]{:S(2)}, u32[]{:S(2)}) %all-to-all-start.3) | async-done | bytes 921632 | tf_op jit(solution)/shard_map/all_to_all | solution.py:69
  194.2 1.6 gather_fusion.3
  195.8 0.2 reshape.139
  196.1 1.2 copy.73
  197.3 28.3 %reduce-scatter.4.cloned.1.call-done = f32[720,360]{1,0:T(8,128)} async-done(((f32[2880,360]{1,0:T(8,128)}), f32[720,360]{1,0:T(8,128)}) %reduce-scatter.4.cloned.1.call-update) | async-done | bytes 1036816
  225.6 2.6 %copy.76 = f32[360,720]{1,0:T(8,128)} copy(f32[360,720]{0,1:T(8,128)} %bitcast.49) | data formatting | bytes 2073600
  (29 shorter events, 1.0 us)
Async XLA Ops:
  14.0 16.8 %copy-start = (bf16[128,2880]{0,1:T(8,128)(2,1)S(1)}, bf16[128,2880]{0,1:T(8,128)(2,1)}, u32[]{:S(2)}) copy-start(bf16[128,2880]{0,1:T(8,128)(2,1)} %param.7) | copy-start | bytes 2211844
  19.0 17.8 %all-to-all-start.1 = ((bf16[8,1,80]{2,1,0:T(2,128)(2,1)}), bf16[8,1,80]{2,1,0:T(2,128)(2,1)S(1)}, u32[]{:S(2)}, u32[]{:S(2)}) async-start(bf16[8,1,80]{2,1,0:T(2,128)(2,1)} %all_to_all.28), calls=%async_computation.1 | async-start | bytes 8192 | tf_op jit(solution)/shard_map/all_to_all | solution.py:52
  36.9 13.6 %all-to-all-start = ((bf16[8,80,360]{2,1,0:T(8,128)(2,1)}), bf16[8,80,360]{2,1,0:T(8,128)(2,1)S(1)}, u32[]{:S(2)}, u32[]{:S(2)}) async-start(bf16[8,80,360]{2,1,0:T(8,128)(2,1)} %broadcast_select_fusion.1), calls=%async_computation | async-start | bytes 983040 | tf_op jit(solution)/shard_map/all_to_all | solution.py:49
  45.4 9.7 %copy-start.1 = (bf16[1,360,720]{2,1,0:T(8,128)(2,1)S(1)}, bf16[1,360,720]{2,1,0:T(8,128)(2,1)}, u32[]{:S(2)}) copy-start(bf16[1,360,720]{2,1,0:T(8,128)(2,1)} %param.13) | copy-start | bytes 1555204
  50.5 49.2 %all-to-all-start.2 = ((bf16[8,80,2880]{2,1,0:T(8,128)(2,1)}), bf16[8,80,2880]{2,1,0:T(8,128)(2,1)}, u32[]{:S(2)}, u32[]{:S(2)}) async-start(bf16[8,80,2880]{2,1,0:T(8,128)(2,1)} %broadcast_select_fusion), calls=%async_computation.2 | async-start | bytes 7536640 | tf_op jit(solution)/shard_map/all_to_all | solution.py:46
  55.1 89.2 %all-gather.3.cloned.1.call-start = ((), (), s32[]{:S(2)}) async-start(), calls=%async_computation.6 | async-start | bytes 5529600 | tf_op jit(solution)/shard_map/all_gather | solution.py:61
  57.9 167.7 %reduce-scatter.4.cloned.1.call-start = ((), (), s32[]{:S(2)}) async-start(), calls=%async_computation.7 | async-start | bytes 5529600
  166.4 9.0 %all-to-all-start.4 = ((f32[8,1,80]{2,1,0:T(1,128)}), f32[8,1,80]{2,1,0:T(1,128)S(1)}, u32[]{:S(2)}, u32[]{:S(2)}) async-start(f32[8,1,80]{2,1,0:T(1,128)} %all_to_all.26), calls=%async_computation.4 | async-start | bytes 8192 | tf_op jit(solution)/shard_map/all_to_all | solution.py:72
  175.3 18.9 %all-to-all-start.3 = ((f32[8,80,360]{2,1,0:T(8,128)}), f32[8,80,360]{2,1,0:T(8,128)S(1)}, u32[]{:S(2)}, u32[]{:S(2)}) async-start(f32[8,80,360]{2,1,0:T(8,128)} %bitcast.16), calls=%async_computation.3 | async-start | bytes 1966080 | tf_op jit(solution)/shard_map/all_to_all | solution.py:69
Sparse Core Ops, SparseCore 0:
  58.0 86.1 all-gather.2
  146.6 78.9 reduce-scatter.3
where the time goes:
time: 236 us; the launch traced here: 235 us
  waiting for transfers between devices  123 us (52%)
  local copies, waits for them, and re-layouts  50.1 us (21%)
  starting transfers between devices  22.1 us (9%)
  matrix products  14.9 us (6%)
  between operations  14.2 us (6%)
  other arithmetic  10.3 us (4%)
    all_to_all x1, waiting for transfers between devices, local(): lax.all_to_all(send_cot.reshape(nexp, cap, width), 'expert', split_axis=0...  41.5 us
    all_gather x1, waiting for transfers between devices, local(): piece = lax.all_gather(local_weight, 'dp', axis=1, tiled=True)  38 us
    unnamed x3, waiting for transfers between devices  28.3 us
    all_gather x1, local copies, waits for them, and re-layouts, local(): piece = lax.all_gather(local_weight, 'dp', axis=1, tiled=True)  11.1 us
    all_to_all x1, waiting for transfers between devices, local(): lax.all_to_all(dhid.reshape(nexp, cap, ffw), 'expert', split_axis=0, conc...  10.4 us
    unnamed x11, local copies, waits for them, and re-layouts  10 us
    dot_general x1, matrix products, weight_terms(): lax.dot_general(hid_recv, gated, (((0,), (0,)), ((), ())), preferred_elem...  6.5 us
    reshape x1, local copies, waits for them, and re-layouts, local(): recv_cot = recv_cot.reshape(slots, width)  5.93 us
  transfers between devices with their start and end apart: 7, of which 5 were waited for; matrix products, arithmetic and copies ran while one was open for 26% of the time, Pallas kernels for 0%

commit v1 on v0

--- a/solution.py
+++ b/solution.py
@@ -1,6 +1,10 @@
+import functools
+
 import jax
 import jax.numpy as jnp
 from jax import lax
+from jax.experimental import pallas as pl
+from jax.experimental.pallas import tpu as pltpu
 from jax.sharding import PartitionSpec as P
 
 
@@ -79,7 +83,369 @@
     return (grad_down, grad_hidden, grad_gates)
 
 
+MESH = pl.DeviceIdType.MESH
+SIB, ALONG_X, ALONG_Y = 1, 2, 4
+
+
+def round_up(size, unit):
+    return -(-size // unit) * unit
+
+
+def token_scale(resp_lengths, advantage, rows):
+    ends = jnp.cumsum(resp_lengths[0])
+    starts = ends - resp_lengths[0]
+    position = jnp.arange(rows, dtype=jnp.int32)
+    inside = (position[:, None] >= starts[None, :]) & (position[:, None] < ends[None, :])
+    ratio = advantage[0] / resp_lengths[0].astype(jnp.float32)
+    return jnp.sum(jnp.where(inside, ratio[None, :], 0.0), axis=1)
+
+
+def exchange_kernel(
+    parts, cot_ref, gh_ref, w_ref, gd_ref, backr_ref,
+    cg, ghr, ght, wfull, part, sendbuf, from_left, from_right, backs,
+    c_send, c_recv, g_send, g_recv, w_send, w_recv, r_send, r_recv, b_send, b_recv,
+):
+    z = lax.axis_index("dp")
+    e = lax.axis_index("expert")
+    core, xpos, ypos = e % 2, (e // 2) % 2, e // 4
+    last = parts - 1
+    rows = cot_ref.shape[1]
+    half = rows // 2
+    low = 2 * z < parts
+
+    def peer(mask):
+        c = 1 - core if mask & 1 else core
+        x = 1 - xpos if mask & 2 else xpos
+        y = 1 - ypos if mask & 4 else ypos
+        return (y * 2 + x) * 2 + c
+
+    barrier = pltpu.get_barrier_semaphore()
+    for mask in range(1, 8):
+        pl.semaphore_signal(barrier, inc=1, device_id=(z, peer(mask)), device_id_type=MESH)
+
+    @pl.when(z > 0)
+    def _():
+        pl.semaphore_signal(barrier, inc=1, device_id=(z - 1, e), device_id_type=MESH)
+
+    @pl.when(z < last)
+    def _():
+        pl.semaphore_signal(barrier, inc=1, device_id=(z + 1, e), device_id_type=MESH)
+
+    pl.semaphore_wait(barrier, 7 + jnp.minimum(z, 1) + jnp.minimum(last - z, 1))
+
+    def remote(src, dst, send, recv, device):
+        return pltpu.make_async_remote_copy(
+            src_ref=src, dst_ref=dst, send_sem=send, recv_sem=recv,
+            device_id=device, device_id_type=MESH,
+        )
+
+    def w_copy(hop, rightward):
+        origin = z - hop if rightward else z + hop
+        side = 0 if rightward else 1
+        src = w_ref if hop == 0 else wfull.at[origin]
+        target = z + 1 if rightward else z - 1
+        return remote(
+            src, wfull.at[origin], w_send.at[side, hop], w_recv.at[side, hop], (target, e)
+        )
+
+    def w_recv_wait(hop, rightward):
+        origin = z - 1 - hop if rightward else z + 1 + hop
+        side = 0 if rightward else 1
+        remote(
+            w_ref, wfull.at[origin], w_send.at[side, hop], w_recv.at[side, hop], (z, peer(SIB))
+        ).wait_recv()
+
+    def w_step(hop):
+        for rightward in (True, False):
+            if hop > 0:
+                come = z >= hop if rightward else z + hop <= last
+
+                @pl.when(come)
+                def _(rightward=rightward):
+                    w_recv_wait(hop - 1, rightward)
+
+            if hop < last:
+                go = (z >= hop) & (z < last) if rightward else (z + hop <= last) & (z > 0)
+
+                @pl.when(go)
+                def _(rightward=rightward):
+                    w_copy(hop, rightward).start()
+
+    def g_copy(mask):
+        p = peer(mask)
+        return remote(gh_ref.at[p], ghr.at[e], g_send.at[mask], g_recv.at[mask], (z, p))
+
+    def chunk_of(step):
+        return jnp.where(low, (z + parts - 1 - step) % parts, (z + 1 + step) % parts)
+
+    def c_own(step, kind, mask):
+        c = chunk_of(step)
+        return remote(
+            cot_ref.at[c], cg.at[c, e], c_send.at[step, kind], c_recv.at[step, kind],
+            (z, peer(mask)),
+        )
+
+    def c_pass(step, kind, source, mask, first=None):
+        c = chunk_of(step)
+        ref = cg.at[c, peer(source)]
+        if first is not None:
+            ref = cg.at[c, peer(source), pl.ds(first, half)]
+        return remote(
+            ref, ref, c_send.at[step, kind], c_recv.at[step, kind], (z, peer(mask))
+        )
+
+    def c_copies(step):
+        return [
+            c_own(step, 0, SIB), c_own(step, 1, ALONG_X), c_own(step, 2, ALONG_Y),
+            c_pass(step, 3, ALONG_X, ALONG_Y, 0),
+            c_pass(step, 4, ALONG_Y, ALONG_X, half),
+            c_pass(step, 5, ALONG_X, SIB), c_pass(step, 6, ALONG_Y, SIB),
+            c_pass(step, 7, ALONG_X | ALONG_Y, SIB),
+        ]
+
+    copies = [c_copies(step) for step in range(parts)]
+
+    w_step(0)
+    for mask in (6, 2, 4, 1, 3, 5, 7):
+        g_copy(mask).start()
+    for kind in (1, 2, 0):
+        copies[0][kind].start()
+    ghr[e] = gh_ref[e]
+    wfull[z] = w_ref[...]
+    for c in range(parts):
+        cg[c, e] = cot_ref[c]
+
+    def gather(step):
+        for kind in (1, 2):
+            copies[step][kind].wait_recv()
+        for kind in (3, 4):
+            copies[step][kind].start()
+        if step + 1 < parts:
+            for kind in (1, 2, 0):
+                copies[step + 1][kind].start()
+        for kind in (5, 6):
+            copies[step][kind].start()
+        for kind in (3, 4):
+            copies[step][kind].wait_recv()
+        copies[step][7].start()
+        for kind in (0, 5, 6, 7):
+            copies[step][kind].wait_recv()
+
+    def r_copy(c, rightward):
+        side = 0 if rightward else 1
+        dst = from_left if rightward else from_right
+        return remote(
+            sendbuf.at[c], dst.at[c], r_send.at[side, c], r_recv.at[side, c],
+            (z + 1 if rightward else z - 1, e),
+        )
+
+    def r_wait(c, rightward):
+        side = 0 if rightward else 1
+        dst = from_left if rightward else from_right
+        remote(
+            sendbuf.at[c], dst.at[c], r_send.at[side, c], r_recv.at[side, c], (z, peer(SIB))
+        ).wait_recv()
+
+    def r_pass(c, rightward):
+        r_wait(c, rightward)
+        came = (from_left if rightward else from_right)[c].astype(jnp.float32)
+        sendbuf[c] = (part[c] + came).astype(sendbuf.dtype)
+        r_copy(c, rightward).start()
+
+    middle = (z > 0) & (z < last)
+
+    for step in range(parts):
+        gather(step)
+        if step == 0:
+            for mask in range(1, 8):
+                g_copy(mask).wait_recv()
+            wide = ghr.shape[2]
+            tall = ght.shape[0]
+            eye = (
+                lax.broadcasted_iota(jnp.int32, (tall, wide), 0)
+                == lax.broadcasted_iota(jnp.int32, (tall, wide), 1)
+            ).astype(jnp.float32).astype(jnp.bfloat16)
+            ght[...] = lax.dot_general(
+                eye, ghr[...].reshape(8 * rows, wide), (((1,), (1,)), ((), ())),
+                preferred_element_type=jnp.float32,
+            ).astype(jnp.bfloat16)
+        c = chunk_of(step)
+
+        @pl.loop(0, part.shape[2] // 256)
+        def _(tile):
+            cols = pl.ds(pl.multiple_of(tile * 256, 256), 256)
+            part[c, :, cols] = jnp.dot(
+                ght[...], cg[c, :, :, cols].reshape(8 * rows, 256),
+                preferred_element_type=jnp.float32,
+            )
+
+        @pl.when((z == 0) & (c > 0))
+        def _():
+            sendbuf[c] = part[c].astype(sendbuf.dtype)
+            r_copy(c, True).start()
+
+        @pl.when((z == last) & (c < last))
+        def _():
+            sendbuf[c] = part[c].astype(sendbuf.dtype)
+            r_copy(c, False).start()
+
+        if step < last:
+            w_step(step + 1)
+        if step == last - 1:
+
+            @pl.when(middle & low)
+            def _():
+                r_pass(last, True)
+
+            @pl.when(middle & jnp.logical_not(low))
+            def _():
+                r_pass(0, False)
+
+    @pl.loop(0, 4)
+    def _(tile):
+        total = None
+        for d in range(parts):
+            term = lax.dot_general(
+                cg[d, pl.ds(tile * 2, 2)].reshape(2 * rows, cg.shape[3]), wfull[d],
+                (((1,), (1,)), ((), ())), preferred_element_type=jnp.float32,
+            )
+            total = term if total is None else total + term
+        backs[pl.ds(tile * 2, 2)] = total.astype(jnp.bfloat16).reshape(2, rows, backs.shape[2])
+
+    def b_copy(mask):
+        p = peer(mask)
+        return remote(backs.at[p], backr_ref.at[e], b_send.at[mask], b_recv.at[mask], (z, p))
+
+    for mask in (6, 2, 4, 7, 3, 5, 1):
+        b_copy(mask).start()
+    backr_ref[e] = backs[e]
+
+    for i in range(last):
+        right, left = last - i, i
+        more_right = middle & (z < right)
+        more_left = middle & (z > left)
+        if i == 0:
+            more_right = more_right & jnp.logical_not(low)
+            more_left = more_left & low
+
+        @pl.when(more_right)
+        def _():
+            r_pass(right, True)
+
+        @pl.when(more_left)
+        def _():
+            r_pass(left, False)
+
+    @pl.when(z > 0)
+    def _():
+        r_wait(z, True)
+        part[z] = part[z] + from_left[z].astype(jnp.float32)
+
+    @pl.when(z < last)
+    def _():
+        r_wait(z, False)
+        part[z] = part[z] + from_right[z].astype(jnp.float32)
+
+    gd_ref[...] = part[z]
+
+    for mask in range(1, 8):
+        b_copy(mask).wait_recv()
+    for mask in range(1, 8):
+        b_copy(mask).wait_send()
+        g_copy(mask).wait_send()
+    for step in range(parts):
+        for copy in copies[step]:
+            copy.wait_send()
+    for hop in range(last):
+
+        @pl.when((z >= hop) & (z < last))
+        def _():
+            w_copy(hop, True).wait_send()
+
+        @pl.when((z + hop <= last) & (z > 0))
+        def _():
+            w_copy(hop, False).wait_send()
+
+    for c in range(parts):
+
+        @pl.when(z < c)
+        def _():
+            r_copy(c, True).wait_send()
+
+        @pl.when(z > c)
+        def _():
+            r_copy(c, False).wait_send()
+
+
+def fused(grad_out, hidden_act, gate_weights, routing, resp_lengths, advantage, w_down):
+    rows, width = grad_out.shape
+    ffw = hidden_act.shape[2]
+    parts = lax.axis_size("dp")
+    cols = width // parts
+    wide = round_up(cols, 256)
+    tall = round_up(ffw, 16)
+    lanes = round_up(ffw, 128)
+    scale = token_scale(resp_lengths, advantage, rows)
+    cotan = (scale[:, None] * grad_out.astype(jnp.float32)).astype(jnp.bfloat16)
+    cot = jnp.pad(
+        cotan.reshape(rows, parts, cols).transpose(1, 0, 2), ((0, 0), (0, 0), (0, wide - cols))
+    )
+    gates = gate_weights.astype(jnp.float32)
+    hidden = hidden_act.astype(jnp.float32)
+    scaled = (gates[:, :, None] * hidden).astype(jnp.bfloat16)
+    named = routing[None] == jnp.arange(8, dtype=jnp.int32)[:, None, None]
+    gh = jnp.sum(
+        jnp.where(named[..., None], scaled[None], jnp.zeros((), jnp.bfloat16)).astype(jnp.float32),
+        axis=2,
+    ).astype(jnp.bfloat16)
+    gh = jnp.pad(gh, ((0, 0), (0, 0), (0, lanes - ffw)))
+    w = jnp.pad(w_down[0], ((0, tall - ffw), (0, wide - cols)))
+    vmem = pl.BlockSpec(memory_space=pltpu.VMEM)
+    dma = pltpu.SemaphoreType.DMA
+    bf16, f32 = jnp.bfloat16, jnp.float32
+    total, back = pl.pallas_call(
+        functools.partial(exchange_kernel, parts),
+        out_shape=(
+            jax.ShapeDtypeStruct((tall, wide), f32),
+            jax.ShapeDtypeStruct((8, rows, tall), bf16),
+        ),
+        in_specs=[vmem] * 3,
+        out_specs=(vmem, vmem),
+        scratch_shapes=[
+            pltpu.VMEM((parts, 8, rows, wide), bf16),
+            pltpu.VMEM((8, rows, lanes), bf16),
+            pltpu.VMEM((tall, 8 * rows), bf16),
+            pltpu.VMEM((parts, tall, wide), bf16),
+            pltpu.VMEM((parts, tall, wide), f32),
+            pltpu.VMEM((parts, tall, wide), bf16),
+            pltpu.VMEM((parts, tall, wide), bf16),
+            pltpu.VMEM((parts, tall, wide), bf16),
+            pltpu.VMEM((8, rows, tall), bf16),
+            dma((parts, 8)), dma((parts, 8)),
+            dma((8,)), dma((8,)),
+            dma((2, parts)), dma((2, parts)),
+            dma((2, parts)), dma((2, parts)),
+            dma((8,)), dma((8,)),
+        ],
+        compiler_params=pltpu.CompilerParams(
+            collective_id=0, has_side_effects=True, vmem_limit_bytes=52 * 1024 * 1024
+        ),
+        cost_estimate=pl.CostEstimate(
+            flops=32 * rows * width * tall, bytes_accessed=8 * rows * width * 2, transcendentals=0
+        ),
+    )(cot, gh, w)
+    grad_down = total[None, :ffw, :cols]
+    back = back[:, :, :ffw].astype(f32)
+    mine = jnp.sum(jnp.where(named[..., None], back[:, :, None, :], 0.0), axis=0)
+    grad_gates = jnp.sum(mine * hidden, axis=2)
+    grad_hidden = gates[:, :, None] * mine
+    return (grad_down, grad_hidden, grad_gates)
+
+
 def solution(mesh):
+    fits = mesh.shape["expert"] == 8 and 2 <= mesh.shape["dp"] <= 4
+    body = fused if fits else local
+
     placed = (
         P(("dp", "expert"), None),
         P(("dp", "expert"), None, None),
@@ -90,7 +456,7 @@
         P("expert", None, "dp"),
     )
     return jax.shard_map(
-        local,
+        body,
         mesh=mesh,
         in_specs=placed,
         out_specs=(

time: 236 us -> 93.9 us (0.40)
  waiting for transfers between devices: 123 us -> 0 us
  Pallas kernels: 0 us -> 79 us
  local copies, waits for them, and re-layouts: 50.1 us -> 6.18 us
  starting transfers between devices: 22.1 us -> 0 us
  matrix products: 14.9 us -> 0 us
  between operations: 14.2 us -> 0.71 us
  other arithmetic: 10.3 us -> 7.66 us
    pallas_call x0 -> x1, Pallas kernels: none -> 79 us  [fused(): pl.pallas_call(functools.partial(exchange_kernel, parts), out_shape=(jax....]
    all_to_all x5 -> x0, waiting for transfers between devices: 57 us -> none  [the longest x1 41.5 us: local(): lax.all_to_all(send_cot.reshape(nexp, cap, width), 'expert', split_axis=0...]
    all_gather x1 -> x0, waiting for transfers between devices: 38 us -> none  [local(): piece = lax.all_gather(local_weight, 'dp', axis=1, tiled=True)]
    unnamed x3 -> x0, waiting for transfers between devices: 28.3 us -> none
    all_to_all x5 -> x0, starting transfers between devices: 21.9 us -> none  [the longest x1 5.17 us: local(): lax.all_to_all(send_gate.reshape(nexp, cap), 'expert', split_axis=0, conc...]
    gather x5 -> x0, local copies, waits for them, and re-layouts: 15.6 us -> none  [the longest x1 4.58 us: local(): cotan[safe // topk]]
    dot_general x3 -> x0, matrix products: 14.9 us -> none  [the longest x1 6.5 us: weight_terms(): lax.dot_general(hid_recv, gated, (((0,), (0,)), ((), ())), preferred_elem...]
    all_gather x1 -> x0, local copies, waits for them, and re-layouts: 11.1 us -> none  [local(): piece = lax.all_gather(local_weight, 'dp', axis=1, tiled=True)]
  transfers between devices with their start and end apart: 7 -> 0, of which waited for: 5 -> 0; matrix products, arithmetic and copies ran while one was open for 26% -> 0% of each run, Pallas kernels for 0% -> 0%
where the time goes in v1:
time: 93.9 us; the launch traced here: 93.6 us
  Pallas kernels  79 us (84%)
  other arithmetic  7.66 us (8%)
  local copies, waits for them, and re-layouts  6.18 us (7%)
    pallas_call x1, Pallas kernels, fused(): pl.pallas_call(functools.partial(exchange_kernel, parts), out_shape=(jax....  79 us
    broadcast_in_dim x1, local copies, waits for them, and re-layouts, fused(): grad_down = total[None, :ffw, :cols]  2.31 us

profile of v1, /device:TPU:0, one launch (start us, length us, event | category | flops | bytes accessed | tf_op | source)
XLA Modules:
  0.0 93.6 jit_solution(13300001721848566437)
XLA Ops:
  0.6 0.8 reduce-window.4
  1.5 0.7 fusion.3
  2.1 0.7 fusion.4
  2.8 0.1 select_reduce_fusion.2
  2.9 0.7 convert_element_type.33
  3.6 0.7 iota_compare_fusion
  4.3 1.1 %fusion = bf16[128,4,360]{0,2,1:T(8,128)(2,1)S(1)} fusion(bf16[128,4,360]{0,2,1:T(8,128)(2,1)} %param.8, f32[128,4]{0,1:T(4,128)S(1)} %convert_element_type.33), kind=kLoop, calls=%fused_computation.7 | loop fusion | flops 552960 | bytes 739328 | tf_op jit(solution)/shard_map/convert_element_type | solution.py:395
  5.3 0.6 select_reduce_fusion.1
  6.0 0.0 copy-start.2
  6.0 0.4 copy.19
  6.3 0.0 copy-start.1
  6.3 1.0 %pad.13.gh_ref = bf16[8,128,384]{2,1,0:T(8,128)(2,1)} pad(bf16[8,128,360]{2,1,0:T(8,128)(2,1)S(1)} %copy.19, bf16[]{:T(256)} %constant.10.clone.1), padding=0_0x0_0x0_24 | pad | bytes 1523714 | tf_op jit(solution)/shard_map/jit(_pad)/pad | solution.py:401
  7.4 0.0 copy-done.2
  7.4 0.1 pad.14.w_ref
  7.4 0.3 copy-done.1
  7.7 0.1 multiply_convert_fusion
  7.9 0.3 copy.18
  8.2 1.0 %pad.12.cot_ref = bf16[4,128,768]{2,1,0:T(8,128)(2,1)} pad(bf16[4,128,720]{2,1,0:T(8,128)(2,1)S(1)} %bitcast.15, bf16[]{:T(256)} %constant.10.clone.1), padding=0_0x0_0x0_48 | pad | bytes 1523714 | tf_op jit(solution)/shard_map/jit(_pad)/pad | solution.py:390
  9.1 79.0 %shard_map.94 = (f32[368,768]{1,0:T(8,128)}, bf16[8,128,368]{2,1,0:T(8,128)(2,1)S(1)}) custom-call(bf16[4,128,768]{2,1,0:T(8,128)(2,1)} %pad.12.cot_ref, bf16[8,128,384]{2,1,0:T(8,128)(2,1)} %pad.13.gh_ref, bf16[368,768]{1,0:T(8,128)(2,1)S(1)} %pad.14.w_ref), custom_call_target="tpu_custom_call" | custom-call | flops 4341104640 | bytes 5898240 | tf_op jit(solution)/shard_map/pallas_call | solution.py:406
  88.1 2.3 %slice_bitcast_fusion = f32[1,360,720]{2,1,0:T(8,128)} fusion(f32[368,768]{1,0:T(8,128)} %get-tuple-element.5), kind=kLoop, calls=%fused_computation.3 | loop fusion | bytes 2073600 | tf_op jit(solution)/shard_map/broadcast_in_dim | solution.py:437
  90.4 0.1 slice_convert_fusion
  90.6 0.5 copy.20
  91.0 0.0 copy-start
  91.0 0.6 select_reduce_fusion
  91.6 0.4 copy-done
  92.0 1.5 %fusion.1 = (f32[128,4]{0,1:T(4,128)}, f32[128,4,360]{0,2,1:T(8,128)}) fusion(f32[128,4,360]{0,2,1:T(8,128)S(1)} %select_reduce_fusion, bf16[128,4,360]{0,2,1:T(8,128)(2,1)S(1)} %copy-done, f32[128,4]{0,1:T(4,128)S(1)} %convert_element_type.33), kind=kLoop, calls=%fused_computation.8 | loop fusion | flops 736768 | bytes 1847296 | tf_op jit(solution)/shard_map/reduce_sum | solution.py:440
Async XLA Ops:
  6.0 1.4 %copy-start.2 = (bf16[1,360,720]{2,1,0:T(8,128)(2,1)S(1)}, bf16[1,360,720]{2,1,0:T(8,128)(2,1)}, u32[]{:S(2)}) copy-start(bf16[1,360,720]{2,1,0:T(8,128)(2,1)} %param.13) | copy-start | bytes 1555204
  6.3 1.4 %copy-start.1 = (bf16[128,2880]{0,1:T(8,128)(2,1)S(1)}, bf16[128,2880]{0,1:T(8,128)(2,1)}, u32[]{:S(2)}) copy-start(bf16[128,2880]{0,1:T(8,128)(2,1)} %param.7) | copy-start | bytes 2211844
  91.0 1.0 %copy-start = (bf16[128,4,360]{0,2,1:T(8,128)(2,1)S(1)}, bf16[128,4,360]{0,2,1:T(8,128)(2,1)}, u32[]{:S(2)}) copy-start(bf16[128,4,360]{0,2,1:T(8,128)(2,1)} %param.8) | copy-start | bytes 1105924

commit v2 on v1

--- a/solution.py
+++ b/solution.py
@@ -91,26 +91,19 @@
     return -(-size // unit) * unit
 
 
-def token_scale(resp_lengths, advantage, rows):
-    ends = jnp.cumsum(resp_lengths[0])
-    starts = ends - resp_lengths[0]
-    position = jnp.arange(rows, dtype=jnp.int32)
-    inside = (position[:, None] >= starts[None, :]) & (position[:, None] < ends[None, :])
-    ratio = advantage[0] / resp_lengths[0].astype(jnp.float32)
-    return jnp.sum(jnp.where(inside, ratio[None, :], 0.0), axis=1)
-
-
 def exchange_kernel(
-    parts, cot_ref, gh_ref, w_ref, gd_ref, backr_ref,
-    cg, ghr, ght, wfull, part, sendbuf, from_left, from_right, backs,
+    parts, len_ref, adv_ref, out_ref, hid_ref, gate_ref, route_ref, w_ref, gd_ref, mine_ref,
+    cg, early, gh, backr, ghr, ght, wfull, part, sendbuf, from_left, from_right, backs,
     c_send, c_recv, g_send, g_recv, w_send, w_recv, r_send, r_recv, b_send, b_recv,
 ):
     z = lax.axis_index("dp")
     e = lax.axis_index("expert")
     core, xpos, ypos = e % 2, (e // 2) % 2, e // 4
     last = parts - 1
-    rows = cot_ref.shape[1]
-    half = rows // 2
+    cols, rows = out_ref.shape[1:]
+    ffw = hid_ref.shape[1]
+    tall = gh.shape[1]
+    half = round_up(cols // 2, 16)
     low = 2 * z < parts
 
     def peer(mask):
@@ -131,6 +124,37 @@
     def _():
         pl.semaphore_signal(barrier, inc=1, device_id=(z + 1, e), device_id_type=MESH)
 
+    wfull[z] = jnp.zeros(wfull.shape[1:], jnp.bfloat16)
+    wfull[z, 0:ffw] = w_ref[...]
+    routes = route_ref[...]
+    gates = gate_ref[...].astype(jnp.float32)
+    scaled = [
+        (gates[k : k + 1] * hid_ref[k].astype(jnp.float32)).astype(jnp.bfloat16)
+        .astype(jnp.float32)
+        for k in range(hid_ref.shape[0])
+    ]
+    for expert in range(8):
+        own = jnp.zeros((ffw, rows), jnp.float32)
+        for k, block in enumerate(scaled):
+            own = jnp.where(routes[k : k + 1] == expert, block, own)
+        own = jnp.concatenate([own, jnp.zeros((tall - ffw, rows), jnp.float32)], axis=0)
+        gh[expert] = own.astype(jnp.bfloat16)
+
+    position = lax.broadcasted_iota(jnp.int32, (8, rows), 1)
+    scale = jnp.zeros((8, rows), jnp.float32)
+    start = 0
+    for s in range(len_ref.shape[1]):
+        length = len_ref[0, s]
+        end = start + length
+        ratio = jnp.full((8, rows), adv_ref[0, s]) / jnp.full(
+            (8, rows), length.astype(jnp.float32)
+        )
+        scale = scale + jnp.where((position >= start) & (position < end), ratio, 0.0)
+        start = end
+    scale = scale[0:1]
+    for c in range(parts):
+        cg[c, e] = (scale * out_ref[c].astype(jnp.float32)).astype(jnp.bfloat16)
+
     pl.semaphore_wait(barrier, 7 + jnp.minimum(z, 1) + jnp.minimum(last - z, 1))
 
     def remote(src, dst, send, recv, device):
@@ -142,7 +166,7 @@
     def w_copy(hop, rightward):
         origin = z - hop if rightward else z + hop
         side = 0 if rightward else 1
-        src = w_ref if hop == 0 else wfull.at[origin]
+        src = wfull.at[origin]
         target = z + 1 if rightward else z - 1
         return remote(
             src, wfull.at[origin], w_send.at[side, hop], w_recv.at[side, hop], (target, e)
@@ -152,7 +176,8 @@
         origin = z - 1 - hop if rightward else z + 1 + hop
         side = 0 if rightward else 1
         remote(
-            w_ref, wfull.at[origin], w_send.at[side, hop], w_recv.at[side, hop], (z, peer(SIB))
+            wfull.at[origin], wfull.at[origin], w_send.at[side, hop], w_recv.at[side, hop],
+            (z, peer(SIB)),
         ).wait_recv()
 
     def w_step(hop):
@@ -173,7 +198,7 @@
 
     def g_copy(mask):
         p = peer(mask)
-        return remote(gh_ref.at[p], ghr.at[e], g_send.at[mask], g_recv.at[mask], (z, p))
+        return remote(gh.at[p], ghr.at[e], g_send.at[mask], g_recv.at[mask], (z, p))
 
     def chunk_of(step):
         return jnp.where(low, (z + parts - 1 - step) % parts, (z + 1 + step) % parts)
@@ -181,7 +206,7 @@
     def c_own(step, kind, mask):
         c = chunk_of(step)
         return remote(
-            cot_ref.at[c], cg.at[c, e], c_send.at[step, kind], c_recv.at[step, kind],
+            cg.at[c, e], cg.at[c, e], c_send.at[step, kind], c_recv.at[step, kind],
             (z, peer(mask)),
         )
 
@@ -189,7 +214,8 @@
         c = chunk_of(step)
         ref = cg.at[c, peer(source)]
         if first is not None:
-            ref = cg.at[c, peer(source), pl.ds(first, half)]
+            count = half if first == 0 else cols - half
+            ref = cg.at[c, peer(source), pl.ds(first, count)]
         return remote(
             ref, ref, c_send.at[step, kind], c_recv.at[step, kind], (z, peer(mask))
         )
@@ -210,10 +236,7 @@
         g_copy(mask).start()
     for kind in (1, 2, 0):
         copies[0][kind].start()
-    ghr[e] = gh_ref[e]
-    wfull[z] = w_ref[...]
-    for c in range(parts):
-        cg[c, e] = cot_ref[c]
+    ghr[e] = gh[e]
 
     def gather(step):
         for kind in (1, 2):
@@ -225,6 +248,8 @@
                 copies[step + 1][kind].start()
         for kind in (5, 6):
             copies[step][kind].start()
+        if step == 0:
+            w_step(1)
         for kind in (3, 4):
             copies[step][kind].wait_recv()
         copies[step][7].start()
@@ -259,24 +284,14 @@
         if step == 0:
             for mask in range(1, 8):
                 g_copy(mask).wait_recv()
-            wide = ghr.shape[2]
-            tall = ght.shape[0]
-            eye = (
-                lax.broadcasted_iota(jnp.int32, (tall, wide), 0)
-                == lax.broadcasted_iota(jnp.int32, (tall, wide), 1)
-            ).astype(jnp.float32).astype(jnp.bfloat16)
-            ght[...] = lax.dot_general(
-                eye, ghr[...].reshape(8 * rows, wide), (((1,), (1,)), ((), ())),
-                preferred_element_type=jnp.float32,
-            ).astype(jnp.bfloat16)
+            ght[...] = jnp.concatenate([ghr[p] for p in range(8)], axis=1)
         c = chunk_of(step)
 
-        @pl.loop(0, part.shape[2] // 256)
-        def _(tile):
-            cols = pl.ds(pl.multiple_of(tile * 256, 256), 256)
-            part[c, :, cols] = jnp.dot(
-                ght[...], cg[c, :, :, cols].reshape(8 * rows, 256),
-                preferred_element_type=jnp.float32,
+        for first in range(0, cols, 256):
+            count = min(256, cols - first)
+            block = jnp.concatenate([cg[c, p, first : first + count] for p in range(8)], axis=1)
+            part[c, :, first : first + count] = lax.dot_general(
+                ght[...], block, (((1,), (1,)), ((), ())), preferred_element_type=jnp.float32
             )
 
         @pl.when((z == 0) & (c > 0))
@@ -289,8 +304,8 @@
             sendbuf[c] = part[c].astype(sendbuf.dtype)
             r_copy(c, False).start()
 
-        if step < last:
-            w_step(step + 1)
+        if 2 <= step < last:
+            w_step(step)
         if step == last - 1:
 
             @pl.when(middle & low)
@@ -301,24 +316,35 @@
             def _():
                 r_pass(0, False)
 
+    far = jnp.where(low, last, 0)
+
+    def back_term(tile, d):
+        pair = jnp.concatenate([cg[d, 2 * tile], cg[d, 2 * tile + 1]], axis=1)
+        return jnp.dot(wfull[d], pair, preferred_element_type=jnp.float32)
+
+    def b_copy(mask):
+        p = peer(mask)
+        return remote(backs.at[p], backr.at[e], b_send.at[mask], b_recv.at[mask], (z, p))
+
     @pl.loop(0, 4)
     def _(tile):
-        total = None
-        for d in range(parts):
-            term = lax.dot_general(
-                cg[d, pl.ds(tile * 2, 2)].reshape(2 * rows, cg.shape[3]), wfull[d],
-                (((1,), (1,)), ((), ())), preferred_element_type=jnp.float32,
-            )
-            total = term if total is None else total + term
-        backs[pl.ds(tile * 2, 2)] = total.astype(jnp.bfloat16).reshape(2, rows, backs.shape[2])
-
-    def b_copy(mask):
-        p = peer(mask)
-        return remote(backs.at[p], backr_ref.at[e], b_send.at[mask], b_recv.at[mask], (z, p))
-
-    for mask in (6, 2, 4, 7, 3, 5, 1):
-        b_copy(mask).start()
-    backr_ref[e] = backs[e]
+        total = back_term(tile, (far + 1) % parts)
+        for i in range(2, parts):
+            total = total + back_term(tile, (far + i) % parts)
+        early[tile] = total
+
+    if last > 1:
+        w_step(last)
+    for mask in (ALONG_X | ALONG_Y, ALONG_X, ALONG_Y, 0):
+        tile = peer(mask) // 2
+        total = early[tile] + back_term(tile, far)
+        total = total.astype(jnp.bfloat16)
+        backs[2 * tile] = total[:, :rows]
+        backs[2 * tile + 1] = total[:, rows:]
+        if mask:
+            b_copy(mask).start()
+        b_copy(mask | SIB).start()
+    backr[e] = backs[e]
 
     for i in range(last):
         right, left = last - i, i
@@ -336,6 +362,14 @@
         def _():
             r_pass(left, False)
 
+    for mask in range(1, 8):
+        b_copy(mask).wait_recv()
+    for k in range(mine_ref.shape[0]):
+        mine = jnp.zeros((tall, rows), jnp.float32)
+        for expert in range(8):
+            mine = jnp.where(routes[k : k + 1] == expert, backr[expert].astype(jnp.float32), mine)
+        mine_ref[k] = mine.astype(jnp.bfloat16)
+
     @pl.when(z > 0)
     def _():
         r_wait(z, True)
@@ -346,10 +380,8 @@
         r_wait(z, False)
         part[z] = part[z] + from_right[z].astype(jnp.float32)
 
-    gd_ref[...] = part[z]
-
-    for mask in range(1, 8):
-        b_copy(mask).wait_recv()
+    gd_ref[...] = part[z][:ffw]
+
     for mask in range(1, 8):
         b_copy(mask).wait_send()
         g_copy(mask).wait_send()
@@ -382,45 +414,33 @@
     ffw = hidden_act.shape[2]
     parts = lax.axis_size("dp")
     cols = width // parts
-    wide = round_up(cols, 256)
     tall = round_up(ffw, 16)
-    lanes = round_up(ffw, 128)
-    scale = token_scale(resp_lengths, advantage, rows)
-    cotan = (scale[:, None] * grad_out.astype(jnp.float32)).astype(jnp.bfloat16)
-    cot = jnp.pad(
-        cotan.reshape(rows, parts, cols).transpose(1, 0, 2), ((0, 0), (0, 0), (0, wide - cols))
-    )
-    gates = gate_weights.astype(jnp.float32)
-    hidden = hidden_act.astype(jnp.float32)
-    scaled = (gates[:, :, None] * hidden).astype(jnp.bfloat16)
-    named = routing[None] == jnp.arange(8, dtype=jnp.int32)[:, None, None]
-    gh = jnp.sum(
-        jnp.where(named[..., None], scaled[None], jnp.zeros((), jnp.bfloat16)).astype(jnp.float32),
-        axis=2,
-    ).astype(jnp.bfloat16)
-    gh = jnp.pad(gh, ((0, 0), (0, 0), (0, lanes - ffw)))
-    w = jnp.pad(w_down[0], ((0, tall - ffw), (0, wide - cols)))
+    topk = routing.shape[1]
     vmem = pl.BlockSpec(memory_space=pltpu.VMEM)
+    smem = pl.BlockSpec(memory_space=pltpu.SMEM)
     dma = pltpu.SemaphoreType.DMA
     bf16, f32 = jnp.bfloat16, jnp.float32
-    total, back = pl.pallas_call(
+    total, mine = pl.pallas_call(
         functools.partial(exchange_kernel, parts),
         out_shape=(
-            jax.ShapeDtypeStruct((tall, wide), f32),
-            jax.ShapeDtypeStruct((8, rows, tall), bf16),
-        ),
-        in_specs=[vmem] * 3,
+            jax.ShapeDtypeStruct((ffw, cols), f32),
+            jax.ShapeDtypeStruct((topk, tall, rows), bf16),
+        ),
+        in_specs=[smem] * 2 + [vmem] * 5,
         out_specs=(vmem, vmem),
         scratch_shapes=[
-            pltpu.VMEM((parts, 8, rows, wide), bf16),
-            pltpu.VMEM((8, rows, lanes), bf16),
+            pltpu.VMEM((parts, 8, cols, rows), bf16),
+            pltpu.VMEM((4, tall, 2 * rows), f32),
+            pltpu.VMEM((8, tall, rows), bf16),
+            pltpu.VMEM((8, tall, rows), bf16),
+            pltpu.VMEM((8, tall, rows), bf16),
             pltpu.VMEM((tall, 8 * rows), bf16),
-            pltpu.VMEM((parts, tall, wide), bf16),
-            pltpu.VMEM((parts, tall, wide), f32),
-            pltpu.VMEM((parts, tall, wide), bf16),
-            pltpu.VMEM((parts, tall, wide), bf16),
-            pltpu.VMEM((parts, tall, wide), bf16),
-            pltpu.VMEM((8, rows, tall), bf16),
+            pltpu.VMEM((parts, tall, cols), bf16),
+            pltpu.VMEM((parts, tall, cols), f32),
+            pltpu.VMEM((parts, tall, cols), bf16),
+            pltpu.VMEM((parts, tall, cols), bf16),
+            pltpu.VMEM((parts, tall, cols), bf16),
+            pltpu.VMEM((8, tall, rows), bf16),
             dma((parts, 8)), dma((parts, 8)),
             dma((8,)), dma((8,)),
             dma((2, parts)), dma((2, parts)),
@@ -433,17 +453,19 @@
         cost_estimate=pl.CostEstimate(
             flops=32 * rows * width * tall, bytes_accessed=8 * rows * width * 2, transcendentals=0
         ),
-    )(cot, gh, w)
-    grad_down = total[None, :ffw, :cols]
-    back = back[:, :, :ffw].astype(f32)
-    mine = jnp.sum(jnp.where(named[..., None], back[:, :, None, :], 0.0), axis=0)
-    grad_gates = jnp.sum(mine * hidden, axis=2)
-    grad_hidden = gates[:, :, None] * mine
+    )(
+        resp_lengths, advantage, grad_out.T.reshape(parts, cols, rows),
+        hidden_act.transpose(1, 2, 0), gate_weights.T, routing.T, w_down[0],
+    )
+    mine = mine[:, :ffw].astype(f32).transpose(2, 0, 1)
+    grad_down = total[None]
+    grad_gates = jnp.sum(mine * hidden_act.astype(f32), axis=2)
+    grad_hidden = gate_weights.astype(f32)[:, :, None] * mine
     return (grad_down, grad_hidden, grad_gates)
 
 
 def solution(mesh):
-    fits = mesh.shape["expert"] == 8 and 2 <= mesh.shape["dp"] <= 4
+    fits = mesh.shape["expert"] == 8 and mesh.shape["dp"] in (2, 4)
     body = fused if fits else local
 
     placed = (

time: 93.9 us -> 80.4 us (0.86)
  Pallas kernels: 79 us -> 72.2 us
  other arithmetic: 7.66 us -> 1.59 us
    pallas_call x1, Pallas kernels: 79 us -> 72.2 us  [fused(): pl.pallas_call(functools.partial(exchange_kernel, parts), out_shape=(jax....]
    unnamed x6 -> x15, local copies, waits for them, and re-layouts: 0.74 us -> 5.69 us
    broadcast_in_dim x1 -> x0, local copies, waits for them, and re-layouts: 2.31 us -> none  [fused(): grad_down = total[None, :ffw, :cols]]
    pad x3 -> x0, local copies, waits for them, and re-layouts: 2.02 us -> none  [the longest x1 1.02 us: fused(): gh = jnp.pad(gh, ((0, 0), (0, 0), (0, lanes - ffw)))]
    convert_element_type x4 -> x1, other arithmetic: 2 us -> 0.01 us  [fused(): grad_hidden = gate_weights.astype(f32)[:, :, None] * mine]
    reduce_sum x4 -> x1, other arithmetic: 2.81 us -> 1.58 us  [fused(): grad_gates = jnp.sum(mine * hidden_act.astype(f32), axis=2)]
where the time goes in v2:
time: 80.4 us; the launch traced here: 80.1 us
  Pallas kernels  72.2 us (90%)
  local copies, waits for them, and re-layouts  5.69 us (7%)
  other arithmetic  1.59 us (2%)
    pallas_call x1, Pallas kernels, fused(): pl.pallas_call(functools.partial(exchange_kernel, parts), out_shape=(jax....  72.2 us
    unnamed x15, local copies, waits for them, and re-layouts  5.69 us

profile of v2, /device:TPU:0, one launch (start us, length us, event | category | flops | bytes accessed | tf_op | source)
XLA Modules:
  0.0 80.1 jit_solution(15958521538201972774)
XLA Ops:
  0.6 0.0 copy-start
  0.6 1.0 %copy-done = bf16[128,4,360]{0,2,1:T(8,128)(2,1)S(1)} copy-done((bf16[128,4,360]{0,2,1:T(8,128)(2,1)S(1)}, bf16[128,4,360]{0,2,1:T(8,128)(2,1)}, u32[]{:S(2)}) %copy-start) | copy-done | bytes 368664
  1.6 0.0 copy-start.1
  1.6 0.7 copy-done.1
  2.3 0.0 copy-start.2
  2.3 1.0 %copy-done.2 = bf16[1,360,720]{2,1,0:T(8,128)(2,1)S(1)} copy-done((bf16[1,360,720]{2,1,0:T(8,128)(2,1)S(1)}, bf16[1,360,720]{2,1,0:T(8,128)(2,1)}, u32[]{:S(2)}) %copy-start.2) | copy-done | bytes 518424
  3.4 0.0 copy-start.3
  3.4 0.7 copy-done.3
  4.0 0.0 copy-start.4
  4.0 0.7 copy-done.4
  4.7 0.0 copy-start.5
  4.7 0.7 copy-done.5
  5.3 72.2 %shard_map.94 = (f32[360,720]{1,0:T(8,128)}, bf16[4,368,128]{2,1,0:T(8,128)(2,1)S(1)}) custom-call(s32[1,4]{1,0:T(1,128)S(1)} %copy-done.4, f32[1,4]{1,0:T(1,128)S(1)} %copy-done.5, bf16[4,720,128]{2,1,0:T(8,128)(2,1)} %bitcast.18, bf16[4,360,128]{2,1,0:T(8,128)(2,1)S(1)} %bitcast.13, bf16[4,128]{1,0:T(4,128)(2,1)S(1)} %bitcast.14, s32[4,128]{1,0:T(4,128)S(1)} %bitcast.16, ...), custom_call_target="tpu_custom_call" | custom-call | flops 4341104640 | bytes 5898240 | tf_op jit(solution)/shard_map/pallas_call | solution.py:423
  77.5 0.0 copy-start.6
  77.5 1.6 %fusion = (f32[128,4]{0,1:T(4,128)}, f32[128,4,360]{0,2,1:T(8,128)}) fusion(bf16[128,4,360]{0,2,1:T(8,128)(2,1)S(1)} %copy-done, bf16[4,368,128]{2,1,0:T(8,128)(2,1)S(1)} %get-tuple-element.6, f32[128,4]{0,1:T(4,128)S(1)} %convert_element_type.7), kind=kLoop, calls=%fused_computation.2 | loop fusion | flops 921088 | bytes 1478656 | tf_op jit(solution)/shard_map/reduce_sum | solution.py:462
  79.1 0.0 copy-done.6
  79.1 1.0 %copy.11 = f32[1,360,720]{2,1,0:T(8,128)} copy(f32[1,360,720]{2,1,0:T(8,128)S(1)} %bitcast.17) | data formatting | bytes 2073600
  (1 shorter events, 0.0 us)
Async XLA Ops:
  0.6 1.0 %copy-start = (bf16[128,4,360]{0,2,1:T(8,128)(2,1)S(1)}, bf16[128,4,360]{0,2,1:T(8,128)(2,1)}, u32[]{:S(2)}) copy-start(bf16[128,4,360]{0,2,1:T(8,128)(2,1)} %param.8) | copy-start | bytes 1105924
  1.6 0.7 copy-start.1
  2.3 1.1 %copy-start.2 = (bf16[1,360,720]{2,1,0:T(8,128)(2,1)S(1)}, bf16[1,360,720]{2,1,0:T(8,128)(2,1)}, u32[]{:S(2)}) copy-start(bf16[1,360,720]{2,1,0:T(8,128)(2,1)} %param.13) | copy-start | bytes 1555204
  3.4 0.7 copy-start.3
  4.0 0.7 copy-start.4
  4.7 0.7 copy-start.5
  77.5 1.6 %copy-start.6 = (f32[360,720]{1,0:T(8,128)S(1)}, f32[360,720]{1,0:T(8,128)}, u32[]{:S(2)}) copy-start(f32[360,720]{1,0:T(8,128)} %get-tuple-element.5) | copy-start | bytes 3110404

commit v3 on v0

--- a/solution.py
+++ b/solution.py
@@ -1,6 +1,10 @@
+import functools
+
 import jax
 import jax.numpy as jnp
 from jax import lax
+from jax.experimental import pallas as pl
+from jax.experimental.pallas import tpu as pltpu
 from jax.sharding import PartitionSpec as P
 
 
@@ -79,7 +83,440 @@
     return (grad_down, grad_hidden, grad_gates)
 
 
+MESH = pl.DeviceIdType.MESH
+SIB, ALONG_X, ALONG_Y = 1, 2, 4
+
+
+def round_up(size, unit):
+    return -(-size // unit) * unit
+
+
+def exchange_kernel(
+    parts, len_hbm, adv_hbm, out_hbm, hid_hbm, gate_hbm, route_hbm, w_hbm, gd_ref, mine_ref,
+    len_ref, adv_ref, out_ref, hid_ref, gate_ref, route_ref, w_ref,
+    cg, early, gh, backr, ghr, ght, wfull, part, sendbuf, from_left, from_right, backs,
+    c_send, c_recv, g_send, g_recv, w_send, w_recv, r_send, r_recv, b_send, b_recv, in_sem,
+):
+    z = lax.axis_index("dp")
+    e = lax.axis_index("expert")
+    core, xpos, ypos = e % 2, (e // 2) % 2, e // 4
+    last = parts - 1
+    cols, rows = out_ref.shape[1:]
+    ffw = hid_ref.shape[1]
+    tall = gh.shape[1]
+    split = min(cols, round_up(cols // 2, 128))
+    spans = ((0, split), (split, cols - split))
+    lanes = (pl.ds(0, split), pl.ds(split, part.shape[2] - split))
+    w_half = round_up(tall // 2, 16)
+    w_rows = (pl.ds(0, w_half), pl.ds(w_half, tall - w_half))
+    units = 2 * parts
+    loads = [
+        pltpu.make_async_copy(src, dst, in_sem.at[i])
+        for i, (src, dst) in enumerate((
+            (w_hbm, w_ref), (route_hbm, route_ref), (gate_hbm, gate_ref), (hid_hbm, hid_ref),
+            (len_hbm, len_ref), (adv_hbm, adv_ref), (out_hbm, out_ref),
+        ))
+    ]
+    for load in loads:
+        load.start()
+    low = 2 * z < parts
+
+    def peer(mask):
+        c = 1 - core if mask & 1 else core
+        x = 1 - xpos if mask & 2 else xpos
+        y = 1 - ypos if mask & 4 else ypos
+        return (y * 2 + x) * 2 + c
+
+    barrier = pltpu.get_barrier_semaphore()
+    for mask in range(1, 8):
+        pl.semaphore_signal(barrier, inc=1, device_id=(z, peer(mask)), device_id_type=MESH)
+
+    @pl.when(z > 0)
+    def _():
+        pl.semaphore_signal(barrier, inc=1, device_id=(z - 1, e), device_id_type=MESH)
+
+    @pl.when(z < last)
+    def _():
+        pl.semaphore_signal(barrier, inc=1, device_id=(z + 1, e), device_id_type=MESH)
+
+    wfull[z] = jnp.zeros(wfull.shape[1:], jnp.bfloat16)
+    loads[0].wait()
+    wfull[z, 0:ffw, 0:cols] = w_ref[...]
+    pl.semaphore_wait(barrier, 7 + jnp.minimum(z, 1) + jnp.minimum(last - z, 1))
+
+    def remote(src, dst, send, recv, device):
+        return pltpu.make_async_remote_copy(
+            src_ref=src, dst_ref=dst, send_sem=send, recv_sem=recv,
+            device_id=device, device_id_type=MESH,
+        )
+
+    def w_copy(hop, h, rightward):
+        origin = z - hop if rightward else z + hop
+        side = 0 if rightward else 1
+        target = z + 1 if rightward else z - 1
+        ref = wfull.at[origin, w_rows[h]]
+        return remote(
+            ref, ref, w_send.at[side, hop, h], w_recv.at[side, hop, h], (target, e)
+        )
+
+    def w_recv_wait(hop, h, rightward):
+        origin = z - 1 - hop if rightward else z + 1 + hop
+        side = 0 if rightward else 1
+        ref = wfull.at[origin, w_rows[h]]
+        remote(
+            ref, ref, w_send.at[side, hop, h], w_recv.at[side, hop, h], (z, peer(SIB))
+        ).wait_recv()
+
+    def w_step(hop, h):
+        for rightward in (True, False):
+            if hop > 0:
+                come = z >= hop if rightward else z + hop <= last
+
+                @pl.when(come)
+                def _(rightward=rightward):
+                    w_recv_wait(hop - 1, h, rightward)
+
+            if hop < last:
+                go = (z >= hop) & (z < last) if rightward else (z + hop <= last) & (z > 0)
+
+                @pl.when(go)
+                def _(rightward=rightward):
+                    w_copy(hop, h, rightward).start()
+
+    def g_copy(mask):
+        p = peer(mask)
+        return remote(gh.at[p], ghr.at[e], g_send.at[mask], g_recv.at[mask], (z, p))
+
+    def chunk_of(step):
+        return jnp.where(low, (z + parts - 1 - step) % parts, (z + 1 + step) % parts)
+
+    def c_copy(unit, kind, source, mask, part_of=None):
+        c, (first, count) = chunk_of(unit // 2), spans[unit % 2]
+        if part_of is not None:
+            near = round_up(count // 2, 16)
+            first, count = (first, near) if part_of == 0 else (first + near, count - near)
+        ref = cg.at[c, peer(source), pl.ds(first, count)]
+        return remote(
+            ref, ref, c_send.at[unit, kind], c_recv.at[unit, kind], (z, peer(mask))
+        )
+
+    def c_copies(unit):
+        return [
+            c_copy(unit, 0, 0, SIB), c_copy(unit, 1, 0, ALONG_X), c_copy(unit, 2, 0, ALONG_Y),
+            c_copy(unit, 3, ALONG_X, ALONG_Y, 0), c_copy(unit, 4, ALONG_Y, ALONG_X, 1),
+            c_copy(unit, 5, ALONG_X, SIB), c_copy(unit, 6, ALONG_Y, SIB),
+            c_copy(unit, 7, ALONG_X | ALONG_Y, SIB),
+        ]
+
+    copies = [c_copies(unit) for unit in range(units)]
+
+    w_step(0, 0)
+    w_step(0, 1)
+
+    for load in loads[1:4]:
+        load.wait()
+    routes = route_ref[...]
+    gates = gate_ref[...].astype(jnp.float32)
+    scaled = [
+        (gates[k : k + 1] * hid_ref[k].astype(jnp.float32)).astype(jnp.bfloat16)
+        .astype(jnp.float32)
+        for k in range(hid_ref.shape[0])
+    ]
+    for expert in range(8):
+        own = jnp.zeros((ffw, rows), jnp.float32)
+        for k, block in enumerate(scaled):
+            own = jnp.where(routes[k : k + 1] == expert, block, own)
+        own = jnp.concatenate([own, jnp.zeros((tall - ffw, rows), jnp.float32)], axis=0)
+        gh[expert] = own.astype(jnp.bfloat16)
+
+    for mask in (6, 2, 4, 1, 3, 5, 7):
+        g_copy(mask).start()
+    ghr[e] = gh[e]
+
+    for load in loads[4:]:
+        load.wait()
+    position = lax.broadcasted_iota(jnp.int32, (8, rows), 1)
+    scale = jnp.zeros((8, rows), jnp.float32)
+    start = 0
+    for s in range(len_ref.shape[1]):
+        length = len_ref[0, s]
+        end = start + length
+        ratio = jnp.full((8, rows), adv_ref[0, s]) / jnp.full(
+            (8, rows), length.astype(jnp.float32)
+        )
+        scale = scale + jnp.where((position >= start) & (position < end), ratio, 0.0)
+        start = end
+    scale = scale[0:1]
+
+    def scale_chunk(step):
+        c = chunk_of(step)
+        cg[c, e] = (scale * out_ref[c].astype(jnp.float32)).astype(jnp.bfloat16)
+
+    scale_chunk(0)
+    for kind in (1, 2, 0):
+        copies[0][kind].start()
+    for step in range(1, parts):
+        scale_chunk(step)
+
+    def gather(unit):
+        for kind in (1, 2):
+            copies[unit][kind].wait_recv()
+        for kind in (3, 4):
+            copies[unit][kind].start()
+        for later in ((1, 2) if unit == 0 else (unit + 2,)):
+            if later < units:
+                for kind in (1, 2, 0):
+                    copies[later][kind].start()
+        for kind in (5, 6):
+            copies[unit][kind].start()
+        if unit == 0:
+            w_step(1, 1)
+        for kind in (3, 4):
+            copies[unit][kind].wait_recv()
+        copies[unit][7].start()
+        for kind in (0, 5, 6, 7):
+            copies[unit][kind].wait_recv()
+
+    def r_copy(c, h, rightward):
+        side = 0 if rightward else 1
+        dst = from_left if rightward else from_right
+        return remote(
+            sendbuf.at[c, :, lanes[h]], dst.at[c, :, lanes[h]],
+            r_send.at[side, c, h], r_recv.at[side, c, h],
+            (z + 1 if rightward else z - 1, e),
+        )
+
+    def r_wait(c, h, rightward):
+        side = 0 if rightward else 1
+        dst = from_left if rightward else from_right
+        remote(
+            sendbuf.at[c, :, lanes[h]], dst.at[c, :, lanes[h]],
+            r_send.at[side, c, h], r_recv.at[side, c, h], (z, peer(SIB)),
+        ).wait_recv()
+
+    def r_pass(c, h, rightward):
+        r_wait(c, h, rightward)
+        came = (from_left if rightward else from_right)[c, :, lanes[h]].astype(jnp.float32)
+        sendbuf[c, :, lanes[h]] = (part[c, :, lanes[h]] + came).astype(sendbuf.dtype)
+        r_copy(c, h, rightward).start()
+
+    def r_first(c, h, rightward):
+        sendbuf[c, :, lanes[h]] = part[c, :, lanes[h]].astype(sendbuf.dtype)
+        r_copy(c, h, rightward).start()
+
+    middle = (z > 0) & (z < last)
+
+    def r_farthest(h, near):
+        @pl.when(middle & (low if near else jnp.logical_not(low)))
+        def _():
+            r_pass(last, h, True)
+
+        @pl.when(middle & (jnp.logical_not(low) if near else low))
+        def _():
+            r_pass(0, h, False)
+
+    w_step(1, 0)
+    for unit in range(units):
+        gather(unit)
+        h = unit % 2
+        if unit == 0:
+            for mask in range(1, 8):
+                g_copy(mask).wait_recv()
+            ght[...] = jnp.concatenate([ghr[p] for p in range(8)], axis=1)
+        c = chunk_of(unit // 2)
+        first, count = spans[h]
+        block = jnp.concatenate([cg[c, p, first : first + count] for p in range(8)], axis=1)
+        part[c, :, first : first + count] = lax.dot_general(
+            ght[...], block, (((1,), (1,)), ((), ())), preferred_element_type=jnp.float32
+        )
+
+        @pl.when((z == 0) & (c > 0))
+        def _():
+            r_first(c, h, True)
+
+        @pl.when((z == last) & (c < last))
+        def _():
+            r_first(c, h, False)
+
+        if last > 2:
+            if unit == 3:
+                w_step(2, 0)
+                r_farthest(0, True)
+            if unit == 4:
+                w_step(2, 1)
+            if unit == 5:
+                r_farthest(1, True)
+
+    def r_rest(h):
+        for i in range(1, last):
+            right, left = last - i, i
+
+            @pl.when(middle & (z < right))
+            def _(right=right):
+                r_pass(right, h, True)
+
+            @pl.when(middle & (z > left))
+            def _(left=left):
+                r_pass(left, h, False)
+
+    if last > 2:
+        r_farthest(0, False)
+        r_rest(0)
+
+    far = jnp.where(low, last, 0)
+
+    def back_term(tile, d):
+        pair = jnp.concatenate([cg[d, 2 * tile], cg[d, 2 * tile + 1]], axis=1)
+        return jnp.dot(wfull[d][:, :cols], pair, preferred_element_type=jnp.float32)
+
+    def b_copy(mask):
+        p = peer(mask)
+        return remote(backs.at[p], backr.at[e], b_send.at[mask], b_recv.at[mask], (z, p))
+
+    @pl.loop(0, 4)
+    def _(tile):
+        total = back_term(tile, (far + 1) % parts)
+        for i in range(2, parts):
+            total = total + back_term(tile, (far + i) % parts)
+        early[tile] = total
+
+    if last > 1:
+        w_step(last, 0)
+        w_step(last, 1)
+    for mask in (ALONG_X | ALONG_Y, ALONG_X, ALONG_Y, 0):
+        tile = peer(mask) // 2
+        total = early[tile] + back_term(tile, far)
+        total = total.astype(jnp.bfloat16)
+        backs[2 * tile] = total[:, :rows]
+        backs[2 * tile + 1] = total[:, rows:]
+        if mask:
+            b_copy(mask).start()
+        b_copy(mask | SIB).start()
+    backr[e] = backs[e]
+
+    if last > 2:
+        r_farthest(1, False)
+        r_rest(1)
+
+    for mask in range(1, 8):
+        b_copy(mask).wait_recv()
+    for k in range(mine_ref.shape[0]):
+        mine = jnp.zeros((tall, rows), jnp.float32)
+        for expert in range(8):
+            mine = jnp.where(routes[k : k + 1] == expert, backr[expert].astype(jnp.float32), mine)
+        mine_ref[k] = mine.astype(jnp.bfloat16)
+
+    for h, (first, count) in enumerate(spans):
+
+        @pl.when(z > 0)
+        def _(h=h):
+            r_wait(z, h, True)
+            part[z, :, lanes[h]] += from_left[z, :, lanes[h]].astype(jnp.float32)
+
+        @pl.when(z < last)
+        def _(h=h):
+            r_wait(z, h, False)
+            part[z, :, lanes[h]] += from_right[z, :, lanes[h]].astype(jnp.float32)
+
+        gd_ref[:, first : first + count] = part[z, 0:ffw, first : first + count]
+
+    for mask in range(1, 8):
+        b_copy(mask).wait_send()
+        g_copy(mask).wait_send()
+    for unit in range(units):
+        for copy in copies[unit]:
+            copy.wait_send()
+    for h in range(2):
+        for hop in range(last):
+
+            @pl.when((z >= hop) & (z < last))
+            def _():
+                w_copy(hop, h, True).wait_send()
+
+            @pl.when((z + hop <= last) & (z > 0))
+            def _():
+                w_copy(hop, h, False).wait_send()
+
+        for c in range(parts):
+
+            @pl.when(z < c)
+            def _():
+                r_copy(c, h, True).wait_send()
+
+            @pl.when(z > c)
+            def _():
+                r_copy(c, h, False).wait_send()
+
+
+def fused(grad_out, hidden_act, gate_weights, routing, resp_lengths, advantage, w_down):
+    rows, width = grad_out.shape
+    ffw = hidden_act.shape[2]
+    parts = lax.axis_size("dp")
+    cols = width // parts
+    tall = round_up(ffw, 16)
+    topk = routing.shape[1]
+    wide = round_up(cols, 128)
+    responses = resp_lengths.shape
+    vmem = pl.BlockSpec(memory_space=pltpu.VMEM)
+    hbm = pl.BlockSpec(memory_space=pl.ANY)
+    dma = pltpu.SemaphoreType.DMA
+    bf16, f32 = jnp.bfloat16, jnp.float32
+    total, mine = pl.pallas_call(
+        functools.partial(exchange_kernel, parts),
+        out_shape=(
+            jax.ShapeDtypeStruct((ffw, cols), f32),
+            jax.ShapeDtypeStruct((topk, tall, rows), bf16),
+        ),
+        in_specs=[hbm] * 7,
+        out_specs=(vmem, vmem),
+        scratch_shapes=[
+            pltpu.SMEM(responses, jnp.int32),
+            pltpu.SMEM(responses, f32),
+            pltpu.VMEM((parts, cols, rows), bf16),
+            pltpu.VMEM((topk, ffw, rows), bf16),
+            pltpu.VMEM((topk, rows), bf16),
+            pltpu.VMEM((topk, rows), jnp.int32),
+            pltpu.VMEM((ffw, cols), bf16),
+            pltpu.VMEM((parts, 8, cols, rows), bf16),
+            pltpu.VMEM((4, tall, 2 * rows), f32),
+            pltpu.VMEM((8, tall, rows), bf16),
+            pltpu.VMEM((8, tall, rows), bf16),
+            pltpu.VMEM((8, tall, rows), bf16),
+            pltpu.VMEM((tall, 8 * rows), bf16),
+            pltpu.VMEM((parts, tall, wide), bf16),
+            pltpu.VMEM((parts, tall, wide), f32),
+            pltpu.VMEM((parts, tall, wide), bf16),
+            pltpu.VMEM((parts, tall, wide), bf16),
+            pltpu.VMEM((parts, tall, wide), bf16),
+            pltpu.VMEM((8, tall, rows), bf16),
+            dma((2 * parts, 8)), dma((2 * parts, 8)),
+            dma((8,)), dma((8,)),
+            dma((2, parts, 2)), dma((2, parts, 2)),
+            dma((2, parts, 2)), dma((2, parts, 2)),
+            dma((8,)), dma((8,)),
+            dma((7,)),
+        ],
+        compiler_params=pltpu.CompilerParams(
+            collective_id=0, has_side_effects=True, vmem_limit_bytes=56 * 1024 * 1024
+        ),
+        cost_estimate=pl.CostEstimate(
+            flops=32 * rows * width * tall, bytes_accessed=8 * rows * width * 2, transcendentals=0
+        ),
+    )(
+        resp_lengths, advantage, grad_out.T.reshape(parts, cols, rows),
+        hidden_act.transpose(1, 2, 0), gate_weights.T, routing.T, w_down[0],
+    )
+    mine = mine[:, :ffw].astype(f32).transpose(2, 0, 1)
+    grad_down = total[None]
+    grad_gates = jnp.sum(mine * hidden_act.astype(f32), axis=2)
+    grad_hidden = gate_weights.astype(f32)[:, :, None] * mine
+    return (grad_down, grad_hidden, grad_gates)
+
+
 def solution(mesh):
+    fits = mesh.shape["expert"] == 8 and mesh.shape["dp"] == 4
+    body = fused if fits else local
+
     placed = (
         P(("dp", "expert"), None),
         P(("dp", "expert"), None, None),
@@ -90,7 +527,7 @@
         P("expert", None, "dp"),
     )
     return jax.shard_map(
-        local,
+        body,
         mesh=mesh,
         in_specs=placed,
         out_specs=(

time: 236 us -> 75.8 us (0.32)
  waiting for transfers between devices: 123 us -> 0 us
  Pallas kernels: 0 us -> 71.3 us
  local copies, waits for them, and re-layouts: 50.1 us -> 1 us
  starting transfers between devices: 22.1 us -> 0 us
  matrix products: 14.9 us -> 0 us
  between operations: 14.2 us -> 0.69 us
  other arithmetic: 10.3 us -> 2.64 us
    pallas_call x0 -> x1, Pallas kernels: none -> 71.3 us  [fused(): pl.pallas_call(functools.partial(exchange_kernel, parts), out_shape=(jax....]
    all_to_all x5 -> x0, waiting for transfers between devices: 57 us -> none  [the longest x1 41.5 us: local(): lax.all_to_all(send_cot.reshape(nexp, cap, width), 'expert', split_axis=0...]
    all_gather x1 -> x0, waiting for transfers between devices: 38 us -> none  [local(): piece = lax.all_gather(local_weight, 'dp', axis=1, tiled=True)]
    unnamed x3 -> x0, waiting for transfers between devices: 28.3 us -> none
    all_to_all x5 -> x0, starting transfers between devices: 21.9 us -> none  [the longest x1 5.17 us: local(): lax.all_to_all(send_gate.reshape(nexp, cap), 'expert', split_axis=0, conc...]
    gather x5 -> x0, local copies, waits for them, and re-layouts: 15.6 us -> none  [the longest x1 4.58 us: local(): cotan[safe // topk]]
    dot_general x3 -> x0, matrix products: 14.9 us -> none  [the longest x1 6.5 us: weight_terms(): lax.dot_general(hid_recv, gated, (((0,), (0,)), ((), ())), preferred_elem...]
    all_gather x1 -> x0, local copies, waits for them, and re-layouts: 11.1 us -> none  [local(): piece = lax.all_gather(local_weight, 'dp', axis=1, tiled=True)]
  transfers between devices with their start and end apart: 7 -> 0, of which waited for: 5 -> 0; matrix products, arithmetic and copies ran while one was open for 26% -> 0% of each run, Pallas kernels for 0% -> 0%
where the time goes in v3:
time: 75.8 us; the launch traced here: 75.6 us
  Pallas kernels  71.3 us (94%)
  other arithmetic  2.64 us (3%)
  local copies, waits for them, and re-layouts  1 us (1%)
    pallas_call x1, Pallas kernels, fused(): pl.pallas_call(functools.partial(exchange_kernel, parts), out_shape=(jax....  71.3 us
    reduce_sum x1, other arithmetic, fused(): grad_gates = jnp.sum(mine * hidden_act.astype(f32), axis=2)  2.64 us

profile of v3, /device:TPU:0, one launch (start us, length us, event | category | flops | bytes accessed | tf_op | source)
XLA Modules:
  0.0 75.6 jit_solution(438616985772786516)
XLA Ops:
  0.6 0.0 copy-start.2
  0.6 0.0 copy-start.1
  0.7 71.3 %shard_map.94 = (f32[360,720]{1,0:T(8,128)}, bf16[4,368,128]{2,1,0:T(8,128)(2,1)}) custom-call(s32[1,4]{1,0:T(1,128)} %len_hbm.1, f32[1,4]{1,0:T(1,128)} %adv_hbm.1, bf16[4,720,128]{2,1,0:T(8,128)(2,1)} %bitcast.16, bf16[4,360,128]{2,1,0:T(8,128)(2,1)} %bitcast.14, bf16[4,128]{1,0:T(4,128)(2,1)} %bitcast.15, s32[4,128]{1,0:T(4,128)} %bitcast.18, ...), custom_call_target="tpu_custom_call" | custom-call | flops 4341104640 | bytes 5898240 | tf_op jit(solution)/shard_map/pallas_call | solution.py:464
  72.0 0.0 copy-start
  72.0 0.0 copy-done.2
  72.0 0.0 copy-done.1
  72.0 2.6 %fusion = (f32[128,4]{0,1:T(4,128)}, f32[128,4,360]{0,2,1:T(8,128)}) fusion(bf16[128,4,360]{0,2,1:T(8,128)(2,1)S(1)} %copy-done.1, bf16[4,368,128]{2,1,0:T(8,128)(2,1)} %get-tuple-element.6, f32[128,4]{0,1:T(4,128)S(1)} %convert_element_type.7), kind=kLoop, calls=%fused_computation.2 | loop fusion | flops 921088 | bytes 1478656 | tf_op jit(solution)/shard_map/reduce_sum | solution.py:511
  74.7 0.0 copy-done
  74.7 1.0 %copy.11 = f32[1,360,720]{2,1,0:T(8,128)} copy(f32[1,360,720]{2,1,0:T(8,128)S(1)} %bitcast.13) | data formatting | bytes 2073600
  (1 shorter events, 0.0 us)
Async XLA Ops:
  0.6 71.4 %copy-start.2 = (bf16[128,4]{0,1:T(4,128)(2,1)S(1)}, bf16[128,4]{0,1:T(4,128)(2,1)}, u32[]{:S(2)}) copy-start(bf16[128,4]{0,1:T(4,128)(2,1)} %param.9) | copy-start | bytes 3076
  0.6 71.4 %copy-start.1 = (bf16[128,4,360]{0,2,1:T(8,128)(2,1)S(1)}, bf16[128,4,360]{0,2,1:T(8,128)(2,1)}, u32[]{:S(2)}) copy-start(bf16[128,4,360]{0,2,1:T(8,128)(2,1)} %param.8) | copy-start | bytes 1105924
  72.0 2.7 %copy-start = (f32[360,720]{1,0:T(8,128)S(1)}, f32[360,720]{1,0:T(8,128)}, u32[]{:S(2)}) copy-start(f32[360,720]{1,0:T(8,128)} %get-tuple-element.5) | copy-start | bytes 3110404

commit v4 on v3

--- a/solution.py
+++ b/solution.py
@@ -95,6 +95,7 @@
     parts, len_hbm, adv_hbm, out_hbm, hid_hbm, gate_hbm, route_hbm, w_hbm, gd_ref, mine_ref,
     len_ref, adv_ref, out_ref, hid_ref, gate_ref, route_ref, w_ref,
     cg, early, gh, backr, ghr, ght, wfull, part, sendbuf, from_left, from_right, backs,
+    wtail, tailpart, tailsend, tail_left, tail_right, turned,
     c_send, c_recv, g_send, g_recv, w_send, w_recv, r_send, r_recv, b_send, b_recv, in_sem,
 ):
     z = lax.axis_index("dp")
@@ -106,9 +107,12 @@
     tall = gh.shape[1]
     split = min(cols, round_up(cols // 2, 128))
     spans = ((0, split), (split, cols - split))
-    lanes = (pl.ds(0, split), pl.ds(split, part.shape[2] - split))
-    w_half = round_up(tall // 2, 16)
+    main = wfull.shape[2]
+    tail = cols - main
+    lanes = (pl.ds(0, split), pl.ds(split, main - split))
+    w_half = round_up((tall * main + tail * tall) // (2 * main), 16)
     w_rows = (pl.ds(0, w_half), pl.ds(w_half, tall - w_half))
+    pieces = ((0,), (1, 2))
     units = 2 * parts
     loads = [
         pltpu.make_async_copy(src, dst, in_sem.at[i])
@@ -139,9 +143,26 @@
     def _():
         pl.semaphore_signal(barrier, inc=1, device_id=(z + 1, e), device_id_type=MESH)
 
-    wfull[z] = jnp.zeros(wfull.shape[1:], jnp.bfloat16)
     loads[0].wait()
-    wfull[z, 0:ffw, 0:cols] = w_ref[...]
+    own_w = jnp.concatenate([w_ref[...], jnp.zeros((tall - ffw, cols), jnp.bfloat16)], axis=0)
+    wfull[z] = own_w[:, :main]
+    chosen = (
+        lax.broadcasted_iota(jnp.int32, (tail, cols), 0) + main
+        == lax.broadcasted_iota(jnp.int32, (tail, cols), 1)
+    ).astype(jnp.float32).astype(jnp.bfloat16)
+    wtail[z] = lax.dot_general(
+        chosen, own_w, (((1,), (1,)), ((), ())), preferred_element_type=jnp.float32
+    ).astype(jnp.bfloat16)
+    eye = (
+        lax.broadcasted_iota(jnp.int32, (tall, tall), 0)
+        == lax.broadcasted_iota(jnp.int32, (tall, tall), 1)
+    ).astype(jnp.float32).astype(jnp.bfloat16)
+
+    def turn(block):
+        return lax.dot_general(
+            eye, block, (((1,), (1,)), ((), ())), preferred_element_type=jnp.float32
+        )
+
     pl.semaphore_wait(barrier, 7 + jnp.minimum(z, 1) + jnp.minimum(last - z, 1))
 
     def remote(src, dst, send, recv, device):
@@ -150,21 +171,24 @@
             device_id=device, device_id_type=MESH,
         )
 
-    def w_copy(hop, h, rightward):
+    def w_piece(origin, q):
+        return wtail.at[origin] if q == 2 else wfull.at[origin, w_rows[q]]
+
+    def w_copy(hop, q, rightward):
         origin = z - hop if rightward else z + hop
         side = 0 if rightward else 1
         target = z + 1 if rightward else z - 1
-        ref = wfull.at[origin, w_rows[h]]
+        ref = w_piece(origin, q)
         return remote(
-            ref, ref, w_send.at[side, hop, h], w_recv.at[side, hop, h], (target, e)
+            ref, ref, w_send.at[side, hop, q], w_recv.at[side, hop, q], (target, e)
         )
 
-    def w_recv_wait(hop, h, rightward):
+    def w_recv_wait(hop, q, rightward):
         origin = z - 1 - hop if rightward else z + 1 + hop
         side = 0 if rightward else 1
-        ref = wfull.at[origin, w_rows[h]]
+        ref = w_piece(origin, q)
         remote(
-            ref, ref, w_send.at[side, hop, h], w_recv.at[side, hop, h], (z, peer(SIB))
+            ref, ref, w_send.at[side, hop, q], w_recv.at[side, hop, q], (z, peer(SIB))
         ).wait_recv()
 
     def w_step(hop, h):
@@ -174,14 +198,16 @@
 
                 @pl.when(come)
                 def _(rightward=rightward):
-                    w_recv_wait(hop - 1, h, rightward)
+                    for q in pieces[h]:
+                        w_recv_wait(hop - 1, q, rightward)
 
             if hop < last:
                 go = (z >= hop) & (z < last) if rightward else (z + hop <= last) & (z > 0)
 
                 @pl.when(go)
                 def _(rightward=rightward):
-                    w_copy(hop, h, rightward).start()
+                    for q in pieces[h]:
+                        w_copy(hop, q, rightward).start()
 
     def g_copy(mask):
         p = peer(mask)
@@ -277,32 +303,41 @@
         for kind in (0, 5, 6, 7):
             copies[unit][kind].wait_recv()
 
-    def r_copy(c, h, rightward):
+    def r_piece(rightward, c, q):
         side = 0 if rightward else 1
-        dst = from_left if rightward else from_right
-        return remote(
-            sendbuf.at[c, :, lanes[h]], dst.at[c, :, lanes[h]],
-            r_send.at[side, c, h], r_recv.at[side, c, h],
-            (z + 1 if rightward else z - 1, e),
-        )
-
-    def r_wait(c, h, rightward):
-        side = 0 if rightward else 1
-        dst = from_left if rightward else from_right
-        remote(
-            sendbuf.at[c, :, lanes[h]], dst.at[c, :, lanes[h]],
-            r_send.at[side, c, h], r_recv.at[side, c, h], (z, peer(SIB)),
-        ).wait_recv()
+        if q == 2:
+            src, dst = tailsend.at[c], (tail_left if rightward else tail_right).at[c]
+        else:
+            src = sendbuf.at[c, :, lanes[q]]
+            dst = (from_left if rightward else from_right).at[c, :, lanes[q]]
+        return src, dst, r_send.at[side, c, q], r_recv.at[side, c, q]
+
+    def r_copy(c, q, rightward):
+        return remote(*r_piece(rightward, c, q), (z + 1 if rightward else z - 1, e))
+
+    def r_wait(c, q, rightward):
+        remote(*r_piece(rightward, c, q), (z, peer(SIB))).wait_recv()
 
     def r_pass(c, h, rightward):
-        r_wait(c, h, rightward)
-        came = (from_left if rightward else from_right)[c, :, lanes[h]].astype(jnp.float32)
-        sendbuf[c, :, lanes[h]] = (part[c, :, lanes[h]] + came).astype(sendbuf.dtype)
-        r_copy(c, h, rightward).start()
+        for q in pieces[h]:
+            r_wait(c, q, rightward)
+            if q == 2:
+                came = (tail_left if rightward else tail_right)[c].astype(jnp.float32)
+                tailsend[c] = (tailpart[c] + came).astype(jnp.bfloat16)
+            else:
+                came = (from_left if rightward else from_right)[c, :, lanes[q]]
+                sendbuf[c, :, lanes[q]] = (
+                    part[c, :, lanes[q]] + came.astype(jnp.float32)
+                ).astype(jnp.bfloat16)
+            r_copy(c, q, rightward).start()
 
     def r_first(c, h, rightward):
-        sendbuf[c, :, lanes[h]] = part[c, :, lanes[h]].astype(sendbuf.dtype)
-        r_copy(c, h, rightward).start()
+        for q in pieces[h]:
+            if q == 2:
+                tailsend[c] = tailpart[c].astype(jnp.bfloat16)
+            else:
+                sendbuf[c, :, lanes[q]] = part[c, :, lanes[q]].astype(jnp.bfloat16)
+            r_copy(c, q, rightward).start()
 
     middle = (z > 0) & (z < last)
 
@@ -329,6 +364,11 @@
         part[c, :, first : first + count] = lax.dot_general(
             ght[...], block, (((1,), (1,)), ((), ())), preferred_element_type=jnp.float32
         )
+        if h == 1:
+            tailpart[c] = lax.dot_general(
+                block[main - first :], ght[...], (((1,), (1,)), ((), ())),
+                preferred_element_type=jnp.float32,
+            )
 
         @pl.when((z == 0) & (c > 0))
         def _():
@@ -367,11 +407,17 @@
 
     def back_term(tile, d):
         pair = jnp.concatenate([cg[d, 2 * tile], cg[d, 2 * tile + 1]], axis=1)
-        return jnp.dot(wfull[d][:, :cols], pair, preferred_element_type=jnp.float32)
+        return jnp.dot(
+            wfull[d], pair[:main], preferred_element_type=jnp.float32
+        ) + jnp.dot(turned[d], pair[main:], preferred_element_type=jnp.float32)
 
     def b_copy(mask):
         p = peer(mask)
         return remote(backs.at[p], backr.at[e], b_send.at[mask], b_recv.at[mask], (z, p))
+
+    for i in range(1, parts):
+        d = (far + i) % parts
+        turned[d] = turn(wtail[d]).astype(jnp.bfloat16)
 
     @pl.loop(0, 4)
     def _(tile):
@@ -383,6 +429,7 @@
     if last > 1:
         w_step(last, 0)
         w_step(last, 1)
+    turned[far] = turn(wtail[far]).astype(jnp.bfloat16)
     for mask in (ALONG_X | ALONG_Y, ALONG_X, ALONG_Y, 0):
         tile = peer(mask) // 2
         total = early[tile] + back_term(tile, far)
@@ -406,19 +453,25 @@
             mine = jnp.where(routes[k : k + 1] == expert, backr[expert].astype(jnp.float32), mine)
         mine_ref[k] = mine.astype(jnp.bfloat16)
 
-    for h, (first, count) in enumerate(spans):
-
-        @pl.when(z > 0)
-        def _(h=h):
-            r_wait(z, h, True)
-            part[z, :, lanes[h]] += from_left[z, :, lanes[h]].astype(jnp.float32)
-
-        @pl.when(z < last)
-        def _(h=h):
-            r_wait(z, h, False)
-            part[z, :, lanes[h]] += from_right[z, :, lanes[h]].astype(jnp.float32)
-
-        gd_ref[:, first : first + count] = part[z, 0:ffw, first : first + count]
+    def r_end(rightward):
+        for q in (0, 1, 2):
+            r_wait(z, q, rightward)
+            if q == 2:
+                came = turn((tail_left if rightward else tail_right)[z])
+                part[z, :, main:cols] += came
+            else:
+                came = (from_left if rightward else from_right)[z, :, lanes[q]]
+                part[z, :, lanes[q]] += came.astype(jnp.float32)
+
+    @pl.when(z > 0)
+    def _():
+        r_end(True)
+
+    @pl.when(z < last)
+    def _():
+        r_end(False)
+
+    gd_ref[...] = part[z, 0:ffw, :]
 
     for mask in range(1, 8):
         b_copy(mask).wait_send()
@@ -426,26 +479,26 @@
     for unit in range(units):
         for copy in copies[unit]:
             copy.wait_send()
-    for h in range(2):
+    for q in range(3):
         for hop in range(last):
 
             @pl.when((z >= hop) & (z < last))
             def _():
-                w_copy(hop, h, True).wait_send()
+                w_copy(hop, q, True).wait_send()
 
             @pl.when((z + hop <= last) & (z > 0))
             def _():
-                w_copy(hop, h, False).wait_send()
+                w_copy(hop, q, False).wait_send()
 
         for c in range(parts):
 
             @pl.when(z < c)
             def _():
-                r_copy(c, h, True).wait_send()
+                r_copy(c, q, True).wait_send()
 
             @pl.when(z > c)
             def _():
-                r_copy(c, h, False).wait_send()
+                r_copy(c, q, False).wait_send()
 
 
 def fused(grad_out, hidden_act, gate_weights, routing, resp_lengths, advantage, w_down):
@@ -455,7 +508,8 @@
     cols = width // parts
     tall = round_up(ffw, 16)
     topk = routing.shape[1]
-    wide = round_up(cols, 128)
+    main = cols // 128 * 128
+    tail = cols - main
     responses = resp_lengths.shape
     vmem = pl.BlockSpec(memory_space=pltpu.VMEM)
     hbm = pl.BlockSpec(memory_space=pl.ANY)
@@ -483,16 +537,22 @@
             pltpu.VMEM((8, tall, rows), bf16),
             pltpu.VMEM((8, tall, rows), bf16),
             pltpu.VMEM((tall, 8 * rows), bf16),
-            pltpu.VMEM((parts, tall, wide), bf16),
-            pltpu.VMEM((parts, tall, wide), f32),
-            pltpu.VMEM((parts, tall, wide), bf16),
-            pltpu.VMEM((parts, tall, wide), bf16),
-            pltpu.VMEM((parts, tall, wide), bf16),
+            pltpu.VMEM((parts, tall, main), bf16),
+            pltpu.VMEM((parts, tall, cols), f32),
+            pltpu.VMEM((parts, tall, main), bf16),
+            pltpu.VMEM((parts, tall, main), bf16),
+            pltpu.VMEM((parts, tall, main), bf16),
             pltpu.VMEM((8, tall, rows), bf16),
+            pltpu.VMEM((parts, tail, tall), bf16),
+            pltpu.VMEM((parts, tail, tall), f32),
+            pltpu.VMEM((parts, tail, tall), bf16),
+            pltpu.VMEM((parts, tail, tall), bf16),
+            pltpu.VMEM((parts, tail, tall), bf16),
+            pltpu.VMEM((parts, tall, tail), bf16),
             dma((2 * parts, 8)), dma((2 * parts, 8)),
             dma((8,)), dma((8,)),
-            dma((2, parts, 2)), dma((2, parts, 2)),
-            dma((2, parts, 2)), dma((2, parts, 2)),
+            dma((2, parts, 3)), dma((2, parts, 3)),
+            dma((2, parts, 3)), dma((2, parts, 3)),
             dma((8,)), dma((8,)),
             dma((7,)),
         ],

time: 75.8 us -> 78.5 us (1.036)
  Pallas kernels: 71.3 us -> 74 us
    pallas_call x1, Pallas kernels: 71.3 us -> 74 us  [fused(): pl.pallas_call(functools.partial(exchange_kernel, parts), out_shape=(jax....]
where the time goes in v4:
time: 78.5 us; the launch traced here: 78.3 us
  Pallas kernels  74 us (94%)
  other arithmetic  2.64 us (3%)
  local copies, waits for them, and re-layouts  1 us (1%)
    pallas_call x1, Pallas kernels, fused(): pl.pallas_call(functools.partial(exchange_kernel, parts), out_shape=(jax....  74 us
    reduce_sum x1, other arithmetic, fused(): grad_gates = jnp.sum(mine * hidden_act.astype(f32), axis=2)  2.64 us

profile of v4, /device:TPU:0, one launch (start us, length us, event | category | flops | bytes accessed | tf_op | source)
XLA Modules:
  0.0 78.3 jit_solution(18020189489628951904)
XLA Ops:
  0.6 0.0 copy-start.2
  0.6 0.0 copy-start.1
  0.7 74.0 %shard_map.94 = (f32[360,720]{1,0:T(8,128)}, bf16[4,368,128]{2,1,0:T(8,128)(2,1)}) custom-call(s32[1,4]{1,0:T(1,128)} %len_hbm.1, f32[1,4]{1,0:T(1,128)} %adv_hbm.1, bf16[4,720,128]{2,1,0:T(8,128)(2,1)} %bitcast.16, bf16[4,360,128]{2,1,0:T(8,128)(2,1)} %bitcast.14, bf16[4,128]{1,0:T(4,128)(2,1)} %bitcast.15, s32[4,128]{1,0:T(4,128)} %bitcast.18, ...), custom_call_target="tpu_custom_call" | custom-call | flops 4341104640 | bytes 5898240 | tf_op jit(solution)/shard_map/pallas_call | solution.py:518
  74.6 0.0 copy-start
  74.6 0.0 copy-done.2
  74.7 0.0 copy-done.1
  74.7 2.6 %fusion = (f32[128,4]{0,1:T(4,128)}, f32[128,4,360]{0,2,1:T(8,128)}) fusion(bf16[128,4,360]{0,2,1:T(8,128)(2,1)S(1)} %copy-done.1, bf16[4,368,128]{2,1,0:T(8,128)(2,1)} %get-tuple-element.6, f32[128,4]{0,1:T(4,128)S(1)} %convert_element_type.7), kind=kLoop, calls=%fused_computation.2 | loop fusion | flops 921088 | bytes 1478656 | tf_op jit(solution)/shard_map/reduce_sum | solution.py:571
  77.3 0.0 copy-done
  77.3 1.0 %copy.11 = f32[1,360,720]{2,1,0:T(8,128)} copy(f32[1,360,720]{2,1,0:T(8,128)S(1)} %bitcast.13) | data formatting | bytes 2073600
  (1 shorter events, 0.0 us)
Async XLA Ops:
  0.6 74.0 %copy-start.2 = (bf16[128,4]{0,1:T(4,128)(2,1)S(1)}, bf16[128,4]{0,1:T(4,128)(2,1)}, u32[]{:S(2)}) copy-start(bf16[128,4]{0,1:T(4,128)(2,1)} %param.9) | copy-start | bytes 3076
  0.6 74.0 %copy-start.1 = (bf16[128,4,360]{0,2,1:T(8,128)(2,1)S(1)}, bf16[128,4,360]{0,2,1:T(8,128)(2,1)}, u32[]{:S(2)}) copy-start(bf16[128,4,360]{0,2,1:T(8,128)(2,1)} %param.8) | copy-start | bytes 1105924
  74.6 2.7 %copy-start = (f32[360,720]{1,0:T(8,128)S(1)}, f32[360,720]{1,0:T(8,128)}, u32[]{:S(2)}) copy-start(f32[360,720]{1,0:T(8,128)} %get-tuple-element.5) | copy-start | bytes 3110404

commit v5 on v3

--- a/solution.py
+++ b/solution.py
@@ -255,25 +255,26 @@
     scale_chunk(0)
     for kind in (1, 2, 0):
         copies[0][kind].start()
+    for kind in (1, 2, 0):
+        copies[1][kind].start()
     for step in range(1, parts):
         scale_chunk(step)
 
-    def gather(unit):
+    def gather_near(unit):
         for kind in (1, 2):
             copies[unit][kind].wait_recv()
-        for kind in (3, 4):
+        for kind in (3, 4, 5, 6):
             copies[unit][kind].start()
-        for later in ((1, 2) if unit == 0 else (unit + 2,)):
-            if later < units:
-                for kind in (1, 2, 0):
-                    copies[later][kind].start()
-        for kind in (5, 6):
-            copies[unit][kind].start()
-        if unit == 0:
-            w_step(1, 1)
+        if unit + 2 < units:
+            for kind in (1, 2, 0):
+                copies[unit + 2][kind].start()
+
+    def gather_far(unit):
         for kind in (3, 4):
             copies[unit][kind].wait_recv()
         copies[unit][7].start()
+
+    def gather_end(unit):
         for kind in (0, 5, 6, 7):
             copies[unit][kind].wait_recv()
 
@@ -316,8 +317,16 @@
             r_pass(0, h, False)
 
     w_step(1, 0)
+    gather_near(0)
+    gather_near(1)
+    w_step(1, 1)
+    gather_far(0)
     for unit in range(units):
-        gather(unit)
+        if unit >= 1 and unit + 2 < units:
+            gather_near(unit + 2)
+        if unit >= 1 and unit + 1 < units:
+            gather_far(unit + 1)
+        gather_end(unit)
         h = unit % 2
         if unit == 0:
             for mask in range(1, 8):
@@ -338,6 +347,9 @@
         def _():
             r_first(c, h, False)
 
+        if unit == 0:
+            gather_near(2)
+            gather_far(1)
         if last > 2:
             if unit == 3:
                 w_step(2, 0)

time: 75.8 us -> 67 us (0.88); the launches traced: 75.6 us -> 65.9 us
  Pallas kernels: 71.3 us -> 61.6 us
    pallas_call x1, Pallas kernels: 71.3 us -> 61.6 us  [fused(): pl.pallas_call(functools.partial(exchange_kernel, parts), out_shape=(jax....]
where the time goes in v5:
time: 67 us; the launch traced here: 65.9 us
  Pallas kernels  61.6 us (92%)
  other arithmetic  2.64 us (4%)
  local copies, waits for them, and re-layouts  1 us (1%)
  between operations  0.69 us (1%)
    pallas_call x1, Pallas kernels, fused(): pl.pallas_call(functools.partial(exchange_kernel, parts), out_shape=(jax....  61.6 us
    reduce_sum x1, other arithmetic, fused(): grad_gates = jnp.sum(mine * hidden_act.astype(f32), axis=2)  2.64 us

profile of v5, /device:TPU:0, one launch (start us, length us, event | category | flops | bytes accessed | tf_op | source)
XLA Modules:
  0.0 65.9 jit_solution(3108127304287774084)
XLA Ops:
  0.6 0.0 copy-start.2
  0.6 0.0 copy-start.1
  0.7 61.6 %shard_map.94 = (f32[360,720]{1,0:T(8,128)}, bf16[4,368,128]{2,1,0:T(8,128)(2,1)}) custom-call(s32[1,4]{1,0:T(1,128)} %len_hbm.1, f32[1,4]{1,0:T(1,128)} %adv_hbm.1, bf16[4,720,128]{2,1,0:T(8,128)(2,1)} %bitcast.16, bf16[4,360,128]{2,1,0:T(8,128)(2,1)} %bitcast.14, bf16[4,128]{1,0:T(4,128)(2,1)} %bitcast.15, s32[4,128]{1,0:T(4,128)} %bitcast.18, ...), custom_call_target="tpu_custom_call" | custom-call | flops 4341104640 | bytes 5898240 | tf_op jit(solution)/shard_map/pallas_call | solution.py:476
  62.3 0.0 copy-start
  62.3 0.0 copy-done.2
  62.3 0.0 copy-done.1
  62.3 2.6 %fusion = (f32[128,4]{0,1:T(4,128)}, f32[128,4,360]{0,2,1:T(8,128)}) fusion(bf16[128,4,360]{0,2,1:T(8,128)(2,1)S(1)} %copy-done.1, bf16[4,368,128]{2,1,0:T(8,128)(2,1)} %get-tuple-element.6, f32[128,4]{0,1:T(4,128)S(1)} %convert_element_type.7), kind=kLoop, calls=%fused_computation.2 | loop fusion | flops 921088 | bytes 1478656 | tf_op jit(solution)/shard_map/reduce_sum | solution.py:523
  64.9 0.0 copy-done
  64.9 1.0 %copy.11 = f32[1,360,720]{2,1,0:T(8,128)} copy(f32[1,360,720]{2,1,0:T(8,128)S(1)} %bitcast.13) | data formatting | bytes 2073600
  (1 shorter events, 0.0 us)
Async XLA Ops:
  0.6 61.6 %copy-start.2 = (bf16[128,4]{0,1:T(4,128)(2,1)S(1)}, bf16[128,4]{0,1:T(4,128)(2,1)}, u32[]{:S(2)}) copy-start(bf16[128,4]{0,1:T(4,128)(2,1)} %param.9) | copy-start | bytes 3076
  0.6 61.6 %copy-start.1 = (bf16[128,4,360]{0,2,1:T(8,128)(2,1)S(1)}, bf16[128,4,360]{0,2,1:T(8,128)(2,1)}, u32[]{:S(2)}) copy-start(bf16[128,4,360]{0,2,1:T(8,128)(2,1)} %param.8) | copy-start | bytes 1105924
  62.3 2.7 %copy-start = (f32[360,720]{1,0:T(8,128)S(1)}, f32[360,720]{1,0:T(8,128)}, u32[]{:S(2)}) copy-start(f32[360,720]{1,0:T(8,128)} %get-tuple-element.5) | copy-start | bytes 3110404

commit v6 on v4

--- a/solution.py
+++ b/solution.py
@@ -281,25 +281,26 @@
     scale_chunk(0)
     for kind in (1, 2, 0):
         copies[0][kind].start()
+    for kind in (1, 2, 0):
+        copies[1][kind].start()
     for step in range(1, parts):
         scale_chunk(step)
 
-    def gather(unit):
+    def gather_near(unit):
         for kind in (1, 2):
             copies[unit][kind].wait_recv()
-        for kind in (3, 4):
+        for kind in (3, 4, 5, 6):
             copies[unit][kind].start()
-        for later in ((1, 2) if unit == 0 else (unit + 2,)):
-            if later < units:
-                for kind in (1, 2, 0):
-                    copies[later][kind].start()
-        for kind in (5, 6):
-            copies[unit][kind].start()
-        if unit == 0:
-            w_step(1, 1)
+        if unit + 2 < units:
+            for kind in (1, 2, 0):
+                copies[unit + 2][kind].start()
+
+    def gather_far(unit):
         for kind in (3, 4):
             copies[unit][kind].wait_recv()
         copies[unit][7].start()
+
+    def gather_end(unit):
         for kind in (0, 5, 6, 7):
             copies[unit][kind].wait_recv()
 
@@ -351,8 +352,16 @@
             r_pass(0, h, False)
 
     w_step(1, 0)
+    gather_near(0)
+    gather_near(1)
+    w_step(1, 1)
+    gather_far(0)
     for unit in range(units):
-        gather(unit)
+        if unit >= 1 and unit + 2 < units:
+            gather_near(unit + 2)
+        if unit >= 1 and unit + 1 < units:
+            gather_far(unit + 1)
+        gather_end(unit)
         h = unit % 2
         if unit == 0:
             for mask in range(1, 8):
@@ -378,6 +387,9 @@
         def _():
             r_first(c, h, False)
 
+        if unit == 0:
+            gather_near(2)
+            gather_far(1)
         if last > 2:
             if unit == 3:
                 w_step(2, 0)

time: 78.5 us -> 65.7 us (0.84)
  Pallas kernels: 74 us -> 61.2 us
    pallas_call x1, Pallas kernels: 74 us -> 61.2 us  [fused(): pl.pallas_call(functools.partial(exchange_kernel, parts), out_shape=(jax....]
where the time goes in v6:
time: 65.7 us; the launch traced here: 65.5 us
  Pallas kernels  61.2 us (93%)
  other arithmetic  2.64 us (4%)
  local copies, waits for them, and re-layouts  1 us (2%)
  between operations  0.69 us (1%)
    pallas_call x1, Pallas kernels, fused(): pl.pallas_call(functools.partial(exchange_kernel, parts), out_shape=(jax....  61.2 us
    reduce_sum x1, other arithmetic, fused(): grad_gates = jnp.sum(mine * hidden_act.astype(f32), axis=2)  2.64 us

profile of v6, /device:TPU:0, one launch (start us, length us, event | category | flops | bytes accessed | tf_op | source)
XLA Modules:
  0.0 65.5 jit_solution(18153473804012306499)
XLA Ops:
  0.6 0.0 copy-start.2
  0.6 0.0 copy-start.1
  0.7 61.2 %shard_map.94 = (f32[360,720]{1,0:T(8,128)}, bf16[4,368,128]{2,1,0:T(8,128)(2,1)}) custom-call(s32[1,4]{1,0:T(1,128)} %len_hbm.1, f32[1,4]{1,0:T(1,128)} %adv_hbm.1, bf16[4,720,128]{2,1,0:T(8,128)(2,1)} %bitcast.16, bf16[4,360,128]{2,1,0:T(8,128)(2,1)} %bitcast.14, bf16[4,128]{1,0:T(4,128)(2,1)} %bitcast.15, s32[4,128]{1,0:T(4,128)} %bitcast.18, ...), custom_call_target="tpu_custom_call" | custom-call | flops 4341104640 | bytes 5898240 | tf_op jit(solution)/shard_map/pallas_call | solution.py:530
  61.8 0.0 copy-start
  61.8 0.0 copy-done.2
  61.9 0.0 copy-done.1
  61.9 2.6 %fusion = (f32[128,4]{0,1:T(4,128)}, f32[128,4,360]{0,2,1:T(8,128)}) fusion(bf16[128,4,360]{0,2,1:T(8,128)(2,1)S(1)} %copy-done.1, bf16[4,368,128]{2,1,0:T(8,128)(2,1)} %get-tuple-element.6, f32[128,4]{0,1:T(4,128)S(1)} %convert_element_type.7), kind=kLoop, calls=%fused_computation.2 | loop fusion | flops 921088 | bytes 1478656 | tf_op jit(solution)/shard_map/reduce_sum | solution.py:583
  64.5 0.0 copy-done
  64.5 1.0 %copy.11 = f32[1,360,720]{2,1,0:T(8,128)} copy(f32[1,360,720]{2,1,0:T(8,128)S(1)} %bitcast.13) | data formatting | bytes 2073600
  (1 shorter events, 0.0 us)
Async XLA Ops:
  0.6 61.2 %copy-start.2 = (bf16[128,4]{0,1:T(4,128)(2,1)S(1)}, bf16[128,4]{0,1:T(4,128)(2,1)}, u32[]{:S(2)}) copy-start(bf16[128,4]{0,1:T(4,128)(2,1)} %param.9) | copy-start | bytes 3076
  0.6 61.2 %copy-start.1 = (bf16[128,4,360]{0,2,1:T(8,128)(2,1)S(1)}, bf16[128,4,360]{0,2,1:T(8,128)(2,1)}, u32[]{:S(2)}) copy-start(bf16[128,4,360]{0,2,1:T(8,128)(2,1)} %param.8) | copy-start | bytes 1105924
  61.8 2.7 %copy-start = (f32[360,720]{1,0:T(8,128)S(1)}, f32[360,720]{1,0:T(8,128)}, u32[]{:S(2)}) copy-start(f32[360,720]{1,0:T(8,128)} %get-tuple-element.5) | copy-start | bytes 3110404
